TPU v7x, 256 devices: a whole 4x4x8 slice. The times are simulated.
256 devices in a mesh: gx: 8 (over x, core), gy: 32 (over z, y).
Axes of the slice: x: 4, y: 4, z: 8, core: 2. Of those that a mesh axis runs over, the one named last changes fastest.
Arguments:
- hidden: bfloat16 [32, 512, 1280], P('gy', 'gx'), may hold values from -6 to 6
- lengths: int32 [32], P('gy'), may hold values from 4 to 16384, as said below
- sink_kv: bfloat16 [32, 2, 4, 1024], P('gy', None, None, 'gx'), may hold values from -12 to 12
- kv_cycle: bfloat16 [32, 2, 4608, 1024], P('gy', None, None, 'gx'), may hold values from -12 to 12
- w_qkv: bfloat16 [1280, 3, 1024], P('gy', None, 'gx'), may hold values from -0.15625 to 0.15625
- s_qk: float32 [1024], P('gx'), may hold values from 0.5 to 16
- w_out: bfloat16 [1024, 1280], P('gx', 'gy'), may hold values from -0.1875 to 0.1875
- alpha_attn: float32 [1280], replicated, may hold values from 0.05 to 0.8
- w_up: bfloat16 [1280, 5120], P('gy', 'gx'), may hold values from -0.15625 to 0.15625
- w_gate: bfloat16 [1280, 5120], P('gy', 'gx'), may hold values from -0.15625 to 0.15625
- s_up: float32 [5120], P('gx'), may hold values from 0.5 to 2
- s_gate: float32 [5120], P('gx'), may hold values from 0.5 to 2
- w_down: bfloat16 [5120, 1280], P('gx', 'gy'), may hold values from -0.078125 to 0.078125
- alpha_mlp: float32 [1280], replicated, may hold values from 0.05 to 0.8
Outputs:
- new_hidden: bfloat16 [32, 512, 1280], P('gy', 'gx')
- new_cycle: bfloat16 [32, 2, 4608, 1024], P('gy', None, None, 'gx')
Inputs may be any that keep to these rules, and one draw needn't show every extreme that they name: `lengths`: exactly 8 requests, chosen by the seed, have 16384 cached positions; the others have fewer than 256.
All inputs are finite; a program needn't handle non-finite values.
Results may differ from a plain program's by a relative error of at most 0.012.
The roundings to bfloat16 on the way count: a program that leaves them out, or rounds other values in their place, can miss the bound.
Values may be sent and summed in bfloat16 or wider, within the bound.
A program may use at most 64 MiB of HBM per device.

v0:
```python
import math

import jax
import jax.numpy as jnp
from jax import lax
from jax.sharding import PartitionSpec as P

HD = 64
SINK = 4
WINDOW = 4096
KEY_BLOCK = 512


def joined_along(pieces, dim):
    pieces = jnp.moveaxis(pieces, 0, dim)
    dims = pieces.shape
    return pieces.reshape(*dims[:dim], dims[dim] * dims[dim + 1], *dims[dim + 2 :])


def copy_for_each(shard, axis):
    copies = jnp.broadcast_to(shard, (lax.axis_size(axis), *shard.shape))
    return lax.all_to_all(copies, axis, split_axis=0, concat_axis=0, tiled=True)


def gathered_copies(shard, axis, dim):
    return joined_along(copy_for_each(shard, axis), dim)


def rows_first(arrays, axis, dims):
    turned = [jnp.moveaxis(a, dim, 0) for a, dim in zip(arrays, dims)]
    both = jnp.concatenate([t.reshape(len(t), -1) for t in turned], axis=1)
    filled, at, gathered = (lax.all_gather(both, axis, axis=0, tiled=True), 0, [])
    for t, dim in zip(turned, dims):
        piece = filled[:, at : at + t[0].size].reshape(-1, *t.shape[1:])
        gathered.append(jnp.moveaxis(piece, 0, dim))
        at += t[0].size
    return tuple(gathered)


def cut_along(shard, dim, peers):
    dims = shard.shape
    pieces = shard.reshape(*dims[:dim], peers, dims[dim] // peers, *dims[dim + 1 :])
    return jnp.moveaxis(pieces, dim, 0)


def summed_on_arrival(shard, axis, dim):
    peers = lax.axis_size(axis)
    pieces = lax.all_to_all(cut_along(shard, dim, peers), axis, 0, 0, tiled=True)
    return jnp.sum(pieces.astype(jnp.float32), axis=0)


def rms_unit(values):
    return values * lax.rsqrt(jnp.mean(values * values, axis=-1, keepdims=True) + 1e-06)


def head_unit(values):
    return values * lax.rsqrt(jnp.sum(values * values, axis=-1, keepdims=True) + 1e-06)


def slot_positions(length, slot_ids, cycle_size, new_count):
    lagging = length + new_count - 1 - SINK - slot_ids
    filled = lagging >= 0
    wrapped = jnp.where(filled, lagging, 0) // cycle_size
    return (SINK + slot_ids + cycle_size * wrapped, filled)


def block_update(running_state, queries, key_block, value_block, visible):
    running, totals, weighted = running_state
    scores = jnp.einsum(
        "qhd,khd->qhk", queries, key_block, preferred_element_type=jnp.float32
    ) * math.sqrt(HD)
    scores = jnp.where(visible[:, None, :], scores, -1e30)
    highest = jnp.maximum(running, jnp.max(scores, axis=-1))
    weights = jnp.where(visible[:, None, :], jnp.exp(scores - highest[:, :, None]), 0.0)
    shrink = jnp.exp(running - highest)
    totals = totals * shrink + jnp.sum(weights, axis=-1)
    weighted = weighted * shrink[:, :, None] + jnp.einsum(
        "qhk,khd->qhd",
        weights.astype(jnp.bfloat16),
        value_block,
        preferred_element_type=jnp.float32,
    )
    return (highest, totals, weighted)


def sink_start(queries, sink_rows):
    heads_here = queries.shape[1]
    sink_keys = sink_rows[0].reshape(-1, heads_here, HD)
    sink_values = sink_rows[1].reshape(-1, heads_here, HD)
    scores = jnp.einsum(
        "qhd,khd->qhk", queries, sink_keys, preferred_element_type=jnp.float32
    ) * math.sqrt(HD)
    highest = jnp.max(scores, axis=-1)
    weights = jnp.exp(scores - highest[:, :, None])
    weighted = jnp.einsum(
        "qhk,khd->qhd",
        weights.astype(jnp.bfloat16),
        sink_values,
        preferred_element_type=jnp.float32,
    )
    return (highest, jnp.sum(weights, axis=-1), weighted)


def cycle_range(
    running_state,
    queries,
    cycle_part,
    base_block,
    length,
    first_block,
    last_block,
    new_count,
    cycle_size,
):
    heads_here = queries.shape[1]
    moments = length + jnp.arange(new_count, dtype=jnp.int32)

    def step_block(number, block_state):
        offset = (number - base_block) * KEY_BLOCK
        key_block = lax.dynamic_slice_in_dim(cycle_part[0], offset, KEY_BLOCK, 0).reshape(
            KEY_BLOCK, heads_here, HD
        )
        value_block = lax.dynamic_slice_in_dim(cycle_part[1], offset, KEY_BLOCK, 0).reshape(
            KEY_BLOCK, heads_here, HD
        )
        slot_ids = number * KEY_BLOCK + jnp.arange(KEY_BLOCK, dtype=jnp.int32)
        positions, filled = slot_positions(length, slot_ids, cycle_size, new_count)
        visible = (
            filled[None, :]
            & (positions[None, :] <= moments[:, None])
            & (positions[None, :] > moments[:, None] - WINDOW)
        )
        return block_update(block_state, queries, key_block, value_block, visible)

    lower = jnp.asarray(first_block, dtype=jnp.int32)
    upper = jnp.asarray(last_block, dtype=jnp.int32)
    return lax.fori_loop(lower, upper, step_block, running_state)


def append_rows(cached, length, fresh):
    cycle_size = cached.shape[1]
    new_count = fresh.shape[1]
    start_slot = (length - SINK) % cycle_size
    extended = jnp.concatenate([cached, cached[:, :new_count]], axis=1)
    extended = lax.dynamic_update_slice_in_dim(extended, fresh, start_slot, 1)
    overflow = start_slot + new_count - cycle_size
    row_ids = jnp.arange(new_count, dtype=jnp.int32)
    leading = jnp.where(
        (row_ids < overflow)[None, :, None], extended[:, cycle_size:], extended[:, :new_count]
    )
    return jnp.concatenate([leading, extended[:, new_count:cycle_size]], axis=1)


def per_device(
    hidden,
    lengths,
    sink_kv,
    kv_cycle,
    w_qkv,
    s_qk,
    w_out,
    alpha_attn,
    w_up,
    w_gate,
    s_up,
    s_gate,
    w_down,
    alpha_mlp,
):
    requests, own_rows, model_width = hidden.shape
    new_count = own_rows * lax.axis_size("gx")
    local_cols = s_qk.shape[0]
    heads_here = local_cols // HD
    cycle_size = kv_cycle.shape[2]
    gathered = gathered_copies(hidden, "gx", 1)
    qkv_full, out_full, up_full, gate_full, down_full = rows_first(
        (w_qkv, w_out, w_up, w_gate, w_down), "gy", (0, 1, 0, 0, 1)
    )
    token_rows = gathered.reshape(requests * new_count, model_width)
    projected = jnp.dot(
        token_rows,
        qkv_full.reshape(model_width, 3 * local_cols),
        preferred_element_type=jnp.float32,
    )
    projected = projected.reshape(requests, new_count, 3, heads_here, HD)
    scale_qk = s_qk.reshape(heads_here, HD)
    queries = (head_unit(projected[:, :, 0]) * scale_qk).astype(jnp.bfloat16)
    keys_new = (head_unit(projected[:, :, 1]) * scale_qk).astype(jnp.bfloat16)
    values_new = projected[:, :, 2].astype(jnp.bfloat16)
    fresh_rows = jnp.stack(
        [
            keys_new.reshape(requests, new_count, local_cols),
            values_new.reshape(requests, new_count, local_cols),
        ],
        axis=1,
    )
    new_cycle = jnp.stack([append_rows(kv_cycle[0], lengths[0], fresh_rows[0])])
    partial_state = sink_start(queries[0], sink_kv[0])
    partial_state = cycle_range(
        partial_state,
        queries[0],
        new_cycle[0],
        0,
        lengths[0],
        0,
        (jnp.minimum(lengths[0] + new_count - SINK, cycle_size) + KEY_BLOCK - 1) // KEY_BLOCK,
        new_count,
        cycle_size,
    )
    outputs = [partial_state[2] / partial_state[1][:, :, None]]
    attended = jnp.stack(outputs).astype(jnp.bfloat16).reshape(requests * new_count, local_cols)
    attn_mixed = jnp.dot(attended, out_full, preferred_element_type=jnp.float32).reshape(
        requests, new_count, model_width
    )
    summed = summed_on_arrival(attn_mixed.astype(jnp.bfloat16), "gx", 1)
    residual = hidden.astype(jnp.float32)
    after_own = rms_unit(residual + alpha_attn * (rms_unit(summed) - residual)).astype(jnp.bfloat16)
    after_all = gathered_copies(after_own, "gx", 1)
    mlp_rows = after_all.reshape(requests * new_count, model_width)
    up_branch = jnp.dot(mlp_rows, up_full, preferred_element_type=jnp.float32) * s_up
    gate_branch = jnp.dot(mlp_rows, gate_full, preferred_element_type=jnp.float32) * s_gate
    active = (up_branch * jax.nn.silu(gate_branch)).astype(jnp.bfloat16)
    lowered = jnp.dot(active, down_full, preferred_element_type=jnp.float32).reshape(
        requests, new_count, model_width
    )
    lowered_own = summed_on_arrival(lowered.astype(jnp.bfloat16), "gx", 1)
    own_wide = after_own.astype(jnp.float32)
    result = rms_unit(own_wide + alpha_mlp * (rms_unit(lowered_own) - own_wide)).astype(
        jnp.bfloat16
    )
    return (result, new_cycle)


def solution(mesh):
    return jax.shard_map(
        per_device,
        mesh=mesh,
        in_specs=(
            P("gy", "gx", None),
            P("gy"),
            P("gy", None, None, "gx"),
            P("gy", None, None, "gx"),
            P("gy", None, "gx"),
            P("gx"),
            P("gx", "gy"),
            P(),
            P("gy", "gx"),
            P("gy", "gx"),
            P("gx"),
            P("gx"),
            P("gx", "gy"),
            P(),
        ),
        out_specs=(P("gy", "gx", None), P("gy", None, None, "gx")),
        check_vma=False,
    )
```

profile of v0, /device:TPU:8, one launch (start us, length us, event | category | flops | bytes accessed | tf_op | source)
XLA Modules:
  0.0 232.9 jit_solution(3977108886242229059)
XLA Ops:
  7.2 0.7 copy-done
  7.9 0.7 constant_dynamic-update-slice_fusion.2
  8.6 0.8 constant_dynamic-update-slice_fusion.1
  9.5 0.8 constant_dynamic-update-slice_fusion
  10.3 0.8 bitcast_dynamic-update-slice_fusion
  11.1 0.7 copy-done.4
  11.8 2.1 broadcast_in_dim.69
  13.9 4.3 %all-to-all-start = ((bf16[8,1,64,1280]{3,2,1,0:T(8,128)(2,1)}), bf16[8,1,64,1280]{3,2,1,0:T(8,128)(2,1)}, u32[]{:S(2)}, u32[]{:S(2)}) async-start(bf16[8,1,64,1280]{3,2,1,0:T(8,128)(2,1)} %broadcast_in_dim.69), calls=%async_computation | async-start | bytes 2621440 | tf_op jit(solution)/shard_map/all_to_all | solution.py:22
  19.1 1.0 slice.77
  20.1 1.8 pad_maximum_fusion
  22.0 15.1 %all-to-all-done = bf16[8,1,64,1280]{3,2,1,0:T(8,128)(2,1)} async-done(((bf16[8,1,64,1280]{3,2,1,0:T(8,128)(2,1)}), bf16[8,1,64,1280]{3,2,1,0:T(8,128)(2,1)}, u32[]{:S(2)}, u32[]{:S(2)}) %all-to-all-start) | async-done | bytes 1310752 | tf_op jit(solution)/shard_map/all_to_all | solution.py:22
  37.0 64.8 %all-gather.2.cloned.1.call-done = bf16[1280,2432]{1,0:T(8,128)(2,1)} async-done(((bf16[40,2432]{1,0:T(8,128)(2,1)}), bf16[1280,2432]{1,0:T(8,128)(2,1)}) %all-gather.2.cloned.1.call-update) | async-done | bytes 6225936 | tf_op jit(solution)/shard_map/all_gather | solution.py:32
  101.9 2.3 %fusion.38 = f32[384,512]{1,0:T(8,128)S(1)} fusion(bf16[512,1280]{1,0:T(8,128)(2,1)} %bitcast.3, bf16[1280,2432]{1,0:T(8,128)(2,1)} %all-gather.2.cloned.1.call-done), kind=kOutput, calls=%fused_computation.49 | convolution fusion | flops 503316480 | bytes 3080192 | tf_op jit(solution)/shard_map/dot_general | solution.py:180
  105.4 0.9 dynamic_update_slice.3
  106.7 2.8 %fusion.56 = (bf16[1,2,4608,128]{3,2,1,0:T(8,128)(2,1)}, bf16[2,4608,128]{2,1,0:T(8,128)(2,1)}) fusion(bf16[2,4096,128]{2,1,0:T(8,128)(2,1)S(1)} %slice.82, bf16[2,512,128]{2,1,0:T(8,128)(2,1)S(1)} %slice_select_fusion), kind=kLoop, calls=%fused_computation.99 | loop fusion | flops 4718592 | bytes 7077888 | tf_op jit(solution)/shard_map/stack | solution.py:197
  109.5 2.9 %copy.33 = bf16[2,4608,128]{1,2,0:T(8,128)(2,1)S(1)} copy(bf16[2,4608,128]{2,1,0:T(8,128)(2,1)} %get-tuple-element.245) | data formatting | bytes 4718592
  112.4 35.6 %while.18 = (s32[]{:T(128)}, f32[512,2]{0,1:T(2,128)S(1)}, f32[512,2]{0,1:T(2,128)S(1)}, f32[512,2,64]{0,2,1:T(8,128)S(1)}, s32[]{:T(128)}, /*index=5*/s32[]{:T(...) while((s32[]{:T(128)}, f32[512,2]{0,1:T(2,128)S(1)}, ...), condition=%wide.region_7.8_spmd.clone, body=%wide.region_4.7_spmd.clone.sunk | while | flops 142225920 | bytes 13579463 | solution.py:137
  112.4 0.7 broadcast_add_fusion.2
  113.1 0.7 iota_add_fusion.3
  114.3 0.6 fusion.84
  114.9 0.6 fusion.85
  115.5 0.8 fusion.86
  116.3 0.7 broadcast_add_fusion.2
  117.0 0.7 iota_add_fusion.3
  118.2 0.6 fusion.84
  118.9 0.6 fusion.85
  119.5 0.8 fusion.86
  120.3 0.7 broadcast_add_fusion.2
  121.0 0.7 iota_add_fusion.3
  122.2 0.6 fusion.84
  122.8 0.6 fusion.85
  123.4 0.8 fusion.86
  124.3 0.7 broadcast_add_fusion.2
  124.9 0.7 iota_add_fusion.3
  126.1 0.6 fusion.84
  127.4 0.8 fusion.86
  128.2 0.7 broadcast_add_fusion.2
  128.9 0.7 iota_add_fusion.3
  130.1 0.6 fusion.84
  131.3 0.8 fusion.86
  132.2 0.7 broadcast_add_fusion.2
  132.8 0.7 iota_add_fusion.3
  134.0 0.6 fusion.84
  135.3 0.8 fusion.86
  136.1 0.7 broadcast_add_fusion.2
  136.8 0.7 iota_add_fusion.3
  138.0 0.6 fusion.84
  138.6 0.6 fusion.85
  139.2 0.8 fusion.86
  140.1 0.7 broadcast_add_fusion.2
  140.7 0.7 iota_add_fusion.3
  141.9 0.6 fusion.84
  143.2 0.8 fusion.86
  144.0 0.7 broadcast_add_fusion.2
  144.7 0.7 iota_add_fusion.3
  145.9 0.6 fusion.84
  147.1 0.8 fusion.86
  148.0 1.5 convolution_convert_fusion.1
  149.5 23.1 %all_to_all.20 = bf16[8,1,64,1280]{3,2,1,0:T(8,128)(2,1)S(1)} all-to-all(bf16[8,1,64,1280]{3,2,1,0:T(8,128)(2,1)S(1)} %bitcast.109), channel_id=1, replica_groups=mesh['gx'=8,'gy'=32] {'gx'}, dimensions={0} | all-to-all | bytes 2621440 | tf_op jit(solution)/shard_map/all_to_all | solution.py:48
  173.5 21.4 %all_to_all.21 = bf16[8,1,64,1280]{3,2,1,0:T(8,128)(2,1)S(1)} all-to-all(bf16[8,1,64,1280]{3,2,1,0:T(8,128)(2,1)S(1)} %broadcast_in_dim.71), channel_id=1, replica_groups=mesh['gx'=8,'gy'=32] {'gx'}, dimensions={0} | all-to-all | bytes 2621440 | tf_op jit(solution)/shard_map/all_to_all | solution.py:22
  194.9 3.7 %fusion.26 = f32[512,640]{1,0:T(8,128)} fusion(bf16[512,1280]{1,0:T(8,128)(2,1)S(1)} %bitcast.116, bf16[1280,2432]{1,0:T(8,128)(2,1)} %all-gather.2.cloned.1.call-done, f32[640]{0:T(1024)S(1)} %copy-done.9), kind=kOutput, calls=%fused_computation.43 | convolution fusion | flops 839188480 | bytes 4262400 | tf_op jit(solution)/shard_map/dot_general | solution.py:221
  198.6 4.7 %convolution_convert_fusion = bf16[512,1280]{1,0:T(8,128)(2,1)S(1)} fusion(bf16[1280,2432]{1,0:T(8,128)(2,1)} %all-gather.2.cloned.1.call-done, bf16[512,1280]{1,0:T(8,128)(2,1)S(1)} %bitcast.117, f32[512,640]{1,0:T(8,128)} %fusion.26, f32[640]{0:T(1024)S(1)} %copy-done.10), kind=kOutput, calls=%fused_computation.31 | convolution fusion | flops 1680670720 | bytes 7211520 | tf_op jit(solution)/shard_map/dot_general | solution.py:223
  203.3 21.4 %all_to_all.22 = bf16[8,1,64,1280]{3,2,1,0:T(8,128)(2,1)S(1)} all-to-all(bf16[8,1,64,1280]{3,2,1,0:T(8,128)(2,1)S(1)} %bitcast.118), channel_id=1, replica_groups=mesh['gx'=8,'gy'=32] {'gx'}, dimensions={0} | all-to-all | bytes 2621440 | tf_op jit(solution)/shard_map/all_to_all | solution.py:48
  225.2 0.8 multiply_convert_fusion
  (122 shorter events, 11.1 us)
Async XLA Ops:
  7.2 0.8 copy-start
  7.2 94.7 %all-gather.2.cloned.1.call-start = ((), (), s32[]{:S(2)}) async-start(), calls=%async_computation.4 | async-start | bytes 6420480 | tf_op jit(solution)/shard_map/all_gather | solution.py:32
  11.1 0.7 copy-start.4
  11.8 7.1 %copy-start.8 = (f32[128]{0:T(128)S(1)}, f32[128]{0:T(128)}, u32[]{:S(2)}) copy-start(f32[128]{0:T(128)} %param.21) | copy-start | bytes 1540
  11.8 7.2 %copy-start.7 = (bf16[1,2,4,128]{3,2,1,0:T(4,128)(2,1)S(1)}, bf16[1,2,4,128]{3,2,1,0:T(4,128)(2,1)}, u32[]{:S(2)}) copy-start(bf16[1,2,4,128]{3,2,1,0:T(4,128)(2,1)} %param.18) | copy-start | bytes 6148
  13.9 23.2 %all-to-all-start = ((bf16[8,1,64,1280]{3,2,1,0:T(8,128)(2,1)}), bf16[8,1,64,1280]{3,2,1,0:T(8,128)(2,1)}, u32[]{:S(2)}, u32[]{:S(2)}) async-start(bf16[8,1,64,1280]{3,2,1,0:T(8,128)(2,1)} %broadcast_in_dim.69), calls=%async_computation | async-start | bytes 2621440 | tf_op jit(solution)/shard_map/all_to_all | solution.py:22
  104.4 0.7 copy-start.2
  109.5 2.9 %copy-start.3 = (bf16[512,2,64]{0,2,1:T(8,128)(2,1)S(1)}, bf16[512,2,64]{0,2,1:T(8,128)(2,1)}, u32[]{:S(2)}) copy-start(bf16[512,2,64]{0,2,1:T(8,128)(2,1)} %copy-done.2) | copy-start | bytes 393220
  149.5 23.5 %copy-start.1 = (bf16[1,64,1280]{2,1,0:T(8,128)(2,1)S(1)}, bf16[1,64,1280]{2,1,0:T(8,128)(2,1)}, u32[]{:S(2)}) copy-start(bf16[1,64,1280]{2,1,0:T(8,128)(2,1)} %param.16) | copy-start | bytes 491524
  149.5 23.5 %copy-start.5 = (f32[1280]{0:T(1024)S(1)}, f32[1280]{0:T(1024)}, u32[]{:S(2)}) copy-start(f32[1280]{0:T(1024)} %param.23) | copy-start | bytes 15364
  173.4 21.5 %copy-start.9 = (f32[640]{0:T(1024)S(1)}, f32[640]{0:T(1024)}, u32[]{:S(2)}) copy-start(f32[640]{0:T(1024)} %param.27) | copy-start | bytes 7684
  194.9 3.7 %copy-start.10 = (f32[640]{0:T(1024)S(1)}, f32[640]{0:T(1024)}, u32[]{:S(2)}) copy-start(f32[640]{0:T(1024)} %param.26) | copy-start | bytes 7684
  203.3 21.7 %copy-start.6 = (f32[1280]{0:T(1024)S(1)}, f32[1280]{0:T(1024)}, u32[]{:S(2)}) copy-start(f32[1280]{0:T(1024)} %param.29) | copy-start | bytes 15364
Sparse Core Ops, SparseCore 0:
  11.9 89.9 all-gather.1
where the time goes:
time: 234 us; the launch traced here: 233 us
  waiting for transfers between devices  79.9 us (34%)
  blocking collectives  65.9 us (28%)
  other arithmetic  27.6 us (12%)
  matrix products  25.4 us (11%)
  between operations  15 us (6%)
  local copies, waits for them, and re-layouts  14 us (6%)
  starting transfers between devices  4.34 us (2%)
    all_gather x1, waiting for transfers between devices, rows_first(): lax.all_gather(both, axis, axis=0, tiled=True)  64.8 us
    all_to_all x2, blocking collectives, summed_on_arrival(): lax.all_to_all(cut_along(shard, dim, peers), axis, 0, 0, tiled=True)  44.5 us
    all_to_all x1, blocking collectives, copy_for_each(): return lax.all_to_all(copies, axis, split_axis=0, concat_axis=0, tiled=True)  21.4 us
    all_to_all x1, waiting for transfers between devices, copy_for_each(): return lax.all_to_all(copies, axis, split_axis=0, concat_axis=0, tiled=True)  15.1 us
    dot_general x9, matrix products, block_update(): jnp.einsum('qhk,khd->qhd', weights.astype(jnp.bfloat16), value_block, pre...  7.14 us
    unnamed x27, local copies, waits for them, and re-layouts  6.88 us
    add x9, other arithmetic, cycle_range(): moments = length + jnp.arange(new_count, dtype=jnp.int32)  5.97 us
    sub x9, other arithmetic, step_block(): moments[:, None] - WINDOW  5.86 us
  transfers between devices with their start and end apart: 2, of which 2 were waited for; matrix products, arithmetic and copies ran while one was open for 2% of the time, Pallas kernels for 0%

commit v1 on v0

v1 whole, which is shorter than its diff:
```python
import functools

import jax
import jax.numpy as jnp
from jax import lax
from jax.experimental import pallas as pl
from jax.experimental.pallas import tpu as pltpu
from jax.sharding import PartitionSpec as P

MESH = pl.DeviceIdType.MESH
BF16 = jnp.bfloat16
F32 = jnp.float32

XC, YC, ZC = 4, 4, 8
D = 1280
HQ = 128
FF = 640
TOK = 512
OWN = 64
PAIR = 128
SHARD = 40
PLANE = SHARD * YC
SINK = 4
WINDOW = 4096
CYCLE = 4608
LONG = 16384
HEAD = 3056
TAIL = 2544
OLD = CYCLE - HEAD + TAIL
NEW_AT = OLD + 16
CHUNK = 256
CHUNKS = 17
KEYS = 3 * PAIR + CHUNK * CHUNKS
FIRST = 13
AWAY = -1e30
EARLY = (0, 1)
LATE = (2, 3, 4, 5)
RIGHT_LAST = (1, 2, 5)


def dot(a, b):
    return jnp.dot(a, b, preferred_element_type=F32)


def dot_nt(a, b):
    return lax.dot_general(a, b, (((1,), (1,)), ((), ())), preferred_element_type=F32)


def rms_unit(values):
    return values * lax.rsqrt(jnp.mean(values * values, axis=-1, keepdims=True) + 1e-06)


def lanes(shape):
    return lax.broadcasted_iota(jnp.int32, shape, len(shape) - 1)


def rows_of(shape):
    return lax.broadcasted_iota(jnp.int32, shape, len(shape) - 2)


def layer_kernel(
    lengths,
    hidden,
    sinks,
    cached,
    w_qkv,
    s_qk,
    w_out,
    alpha_attn,
    w_up,
    w_gate,
    s_up,
    s_gate,
    w_down,
    alpha_mlp,
    result,
    fresh,
    g_qkv,
    g_out,
    g_ff,
    g_down,
    edge_a,
    edge_b,
    tokens,
    keys,
    values,
    queries,
    scores,
    partial,
    kept,
    to_sib,
    from_sib,
    to_owner,
    from_peer,
    after,
    local_sem,
    tok_send,
    tok_recv,
    shard_send,
    shard_recv,
    ring_send,
    ring_recv,
    quarter_send,
    quarter_recv,
    sib_send,
    sib_recv,
    sum_send,
    sum_recv,
):
    gx = lax.axis_index("gx")
    gy = lax.axis_index("gy")
    x, c = gx // 2, lax.rem(gx, 2)
    z, y = gy // YC, lax.rem(gy, YC)

    def device(dx=0, other=False, dz=0, dy=0):
        core = 1 - c if other else c
        return (
            lax.rem(x + dx, XC) * 2 + core,
            lax.rem(z + dz, ZC) * YC + lax.rem(y + dy, YC),
        )

    sibling = device(other=True)
    along_x = {d: device(dx=d) for d in (1, 2, 3)}
    along_y = {d: device(dy=d) for d in (1, 2, 3)}
    right, left = device(dz=1), device(dz=ZC - 1)
    everyone = [sibling, *along_x.values(), *along_y.values(), right, left]
    gate_sem = pltpu.get_barrier_semaphore()
    for peer in everyone:
        pl.semaphore_signal(gate_sem, inc=1, device_id=peer, device_id_type=MESH)

    sent = []

    def remote(src, dst, send, recv, to):
        return pltpu.make_async_remote_copy(
            src_ref=src, dst_ref=dst, send_sem=send, recv_sem=recv, device_id=to, device_id_type=MESH
        )

    def go(copy):
        copy.start()
        sent.append(copy)

    def block_of(g):
        return pl.ds(pl.multiple_of(g * OWN, OWN), OWN)

    own_in = pltpu.make_async_copy(hidden.at[0], tokens.at[block_of(gx)], local_sem.at[0])
    own_in.start()
    loads = []
    for kind, store in ((0, keys), (1, values)):
        for n, (src, at, count) in enumerate(
            ((HEAD, 0, CYCLE - HEAD), (0, CYCLE - HEAD, TAIL))
        ):
            loads.append(
                pltpu.make_async_copy(
                    cached.at[0, kind, pl.ds(src, count)],
                    store.at[pl.ds(at, count), pl.ds(0, HQ)],
                    local_sem.at[1 + 2 * kind + n],
                )
            )
    for load in loads:
        load.start()

    odd = lax.rem(y, 2)
    main_rows = pl.ds(
        pl.multiple_of(z * PLANE + (y // 2) * (2 * SHARD) + odd * 48, 16), 32
    )

    def cut(wide):
        main = jnp.where(odd == 1, wide[8:40], wide[0:32]).astype(BF16)
        edge = jnp.concatenate([wide[32:40], wide[0:8]], axis=0).astype(BF16)
        return main, edge

    main, edge = cut(w_qkv[...].astype(F32))
    g_qkv[main_rows, :] = main
    edge_a[y] = edge

    pl.semaphore_wait(gate_sem, len(everyone))

    def shard_copies(n, src_dst):
        return [
            remote(src_dst, src_dst, shard_send.at[n, d - 1], shard_recv.at[n, d - 1], along_y[d])
            for d in (1, 2, 3)
        ]

    first_wave = shard_copies(0, g_qkv.at[main_rows]) + shard_copies(1, edge_a.at[y])
    for copy in first_wave:
        go(copy)

    own_in.wait()

    def token_copy(buffer, phase, d):
        piece = buffer.at[block_of(gx)]
        to = sibling if d == 0 else along_x[d]
        return remote(piece, piece, tok_send.at[phase, d], tok_recv.at[phase, d], to)

    def token_pass_on(buffer, phase, d):
        came = block_of(lax.rem(x + XC - d, XC) * 2 + c)
        direct = remote(
            buffer.at[came], buffer.at[came], tok_send.at[phase, d], tok_recv.at[phase, d], along_x[d]
        )
        direct.wait_recv()
        go(
            remote(
                buffer.at[came],
                buffer.at[came],
                tok_send.at[phase, 3 + d],
                tok_recv.at[phase, 3 + d],
                sibling,
            )
        )

    def token_from_sibling(buffer, phase, d):
        block = buffer.at[block_of(lax.rem(x + XC - d, XC) * 2 + 1 - c)]
        n = 0 if d == 0 else 3 + d
        remote(block, block, tok_send.at[phase, n], tok_recv.at[phase, n], sibling).wait_recv()

    for d in (1, 3, 2, 0):
        go(token_copy(tokens, 0, d))

    def one_hot(n):
        return jnp.where(rows_of((n, n)) == lanes((n, n)), 1.0, 0.0).astype(BF16)

    turned = dot_nt(one_hot(SHARD), w_out[...])
    main, edge = cut(turned)
    g_out[main_rows, :] = main
    edge_b[y, :, 0:HQ] = edge
    up_wide = w_up[...].astype(F32)
    gate_wide = w_gate[...].astype(F32)
    for b in range(5):
        cols = slice(b * HQ, b * HQ + HQ)
        main, edge = cut(jnp.concatenate([up_wide[:, cols], gate_wide[:, cols]], axis=1))
        g_ff[b, main_rows, :] = main
        edge_b[y, :, HQ + 256 * b : HQ + 256 * (b + 1)] = edge
    main, edge = cut(dot_nt(one_hot(SHARD), w_down[...]))
    g_down[main_rows, :] = main
    edge_b[y, :, HQ + 2 * FF :] = edge
    second_wave = (
        shard_copies(2, edge_b.at[y])
        + shard_copies(3, g_ff.at[:, main_rows])
        + shard_copies(4, g_out.at[main_rows])
        + shard_copies(5, g_down.at[main_rows])
    )
    for copy in second_wave:
        go(copy)

    def plane(zz):
        return pl.ds(pl.multiple_of(zz * PLANE, 32), PLANE)

    def part_ref(part, zz):
        if part == 0:
            return g_qkv.at[plane(zz), pl.ds(0, HQ)]
        if part == 1:
            return g_qkv.at[plane(zz), pl.ds(HQ, 2 * HQ)]
        if part == 2:
            return g_ff.at[y, plane(zz)]
        if part == 3:
            return g_ff.at[4, plane(zz)]
        if part == 4:
            return g_out.at[plane(zz)]
        return g_down.at[plane(zz)]

    def last_step(part, way):
        return 4 if (part in RIGHT_LAST) == (way == 0) else 3

    def ring_copy(part, way, step, arriving):
        back = step if arriving else step - 1
        zz = lax.rem(z + ZC - back, ZC) if way == 0 else lax.rem(z + back, ZC)
        piece = part_ref(part, zz)
        return remote(
            piece,
            piece,
            ring_send.at[part, way, step - 1],
            ring_recv.at[part, way, step - 1],
            right if way == 0 else left,
        ), zz

    def quarter_copies(way, step, zz):
        n = step - 1 if way == 0 else 4 + step - 1
        piece = g_ff.at[y, plane(zz)]
        return [
            remote(piece, piece, quarter_send.at[n, d - 1], quarter_recv.at[n, d - 1], along_y[d])
            for d in (1, 2, 3)
        ]

    def ring_stage(parts, step):
        for part in parts:
            for way in (0, 1):
                if 1 <= step - 1 <= last_step(part, way):
                    copy, zz = ring_copy(part, way, step - 1, True)
                    copy.wait_recv()
                if step <= last_step(part, way):
                    go(ring_copy(part, way, step, False)[0])
                if 1 <= step - 1 <= last_step(part, way) and part == 2:
                    for copy in quarter_copies(way, step - 1, zz):
                        go(copy)

    def merge(ref, edges, col, width):
        for pair in (0, 1):
            low = edges[2 * pair, :, col : col + width].astype(F32)
            high = edges[2 * pair + 1, :, col : col + width].astype(F32)
            at = pl.multiple_of(z * PLANE + pair * 2 * SHARD + 32, 16)
            ref[pl.ds(at, 16), :] = jnp.concatenate([low[0:8], high[8:16]], axis=0).astype(BF16)

    def rows_from(d):
        yy = lax.rem(y + YC - d, YC)
        at = z * PLANE + (yy // 2) * (2 * SHARD) + lax.rem(yy, 2) * 48
        return yy, pl.ds(pl.multiple_of(at, 16), 32)

    def shard_arrived(n, ref_of):
        for d in (1, 2, 3):
            yy, rows = rows_from(d)
            piece = ref_of(yy, rows)
            remote(
                piece, piece, shard_send.at[n, d - 1], shard_recv.at[n, d - 1], along_y[d]
            ).wait_recv()

    shard_arrived(0, lambda yy, rows: g_qkv.at[rows])
    shard_arrived(1, lambda yy, rows: edge_a.at[yy])
    merge(g_qkv, edge_a, 0, 3 * HQ)
    ring_stage(EARLY, 1)

    length = lengths[0]

    def key_bias(n, carry):
        at = pl.multiple_of(n * PAIR, PAIR)
        row = rows_of((PAIR, HQ)) + at
        slot = jnp.where(row < CYCLE - HEAD, row + HEAD, row - (CYCLE - HEAD))
        lag = length - 1 - SINK - slot
        turns = (
            jnp.where(lag >= CYCLE, 1, 0)
            + jnp.where(lag >= 2 * CYCLE, 1, 0)
            + jnp.where(lag >= 3 * CYCLE, 1, 0)
        )
        held = SINK + slot + CYCLE * turns
        old = (lag >= 0) & (held >= length - WINDOW) & (row < OLD + 12)
        seen = old | ((row >= OLD + 12) & (row < NEW_AT + TOK))
        keys[pl.ds(at, PAIR), HQ : 2 * HQ] = jnp.where(seen, 0.0, AWAY).astype(BF16)
        values[pl.ds(at, PAIR), HQ : 2 * HQ] = jnp.ones((PAIR, HQ), BF16)
        return carry

    lax.fori_loop(0, KEYS // PAIR, key_bias, 0)
    spare = KEYS - NEW_AT - TOK
    for kind, store in ((0, keys), (1, values)):
        store[OLD:NEW_AT, 0:HQ] = sinks[kind]
        store[NEW_AT + TOK :, 0:HQ] = jnp.zeros((spare, HQ), BF16)

    shard_arrived(2, lambda yy, rows: edge_b.at[yy])
    shard_arrived(3, lambda yy, rows: g_ff.at[:, rows])
    shard_arrived(4, lambda yy, rows: g_out.at[rows])
    shard_arrived(5, lambda yy, rows: g_down.at[rows])
    merge(g_out, edge_b, 0, HQ)
    for b in range(5):
        merge(g_ff.at[b], edge_b, HQ + 256 * b, 256)
    merge(g_down, edge_b, HQ + 2 * FF, FF)
    ring_stage(LATE, 1)
    ring_stage(EARLY, 2)
    for d in (1, 3):
        token_pass_on(tokens, 0, d)
    ring_stage(EARLY, 3)
    token_pass_on(tokens, 0, 2)
    ring_stage(LATE, 2)
    ring_stage(EARLY, 4)
    for d in (0, 1, 2, 3):
        token_from_sibling(tokens, 0, d)
    for step in (4,):
        for part in EARLY:
            for way in (0, 1):
                if last_step(part, way) == step:
                    ring_copy(part, way, step, True)[0].wait_recv()
    for load in loads:
        load.wait()

    low_head = lanes((PAIR, HQ)) < 64

    def head_unit(v):
        squares = v * v
        low = jnp.sum(jnp.where(low_head, squares, 0.0), axis=-1, keepdims=True)
        high = jnp.sum(jnp.where(low_head, 0.0, squares), axis=-1, keepdims=True)
        return v * jnp.where(low_head, lax.rsqrt(low + 1e-06), lax.rsqrt(high + 1e-06))

    def project(n, carry):
        at = pl.multiple_of(n * PAIR, PAIR)
        qkv = dot(tokens[pl.ds(at, PAIR), :], g_qkv[...])
        scale = s_qk[...]
        q = (head_unit(qkv[:, 0:HQ]) * scale).astype(BF16)
        queries[pl.ds(at, PAIR), :] = (q.astype(F32) * 8.0).astype(BF16)
        k = (head_unit(qkv[:, HQ : 2 * HQ]) * scale).astype(BF16)
        v = qkv[:, 2 * HQ :].astype(BF16)
        to = pl.ds(pl.multiple_of(NEW_AT + at, 16), PAIR)
        keys[to, 0:HQ] = k
        values[to, 0:HQ] = v
        fresh[0, 0, pl.ds(at, PAIR), :] = k
        fresh[0, 1, pl.ds(at, PAIR), :] = v
        return carry

    lax.fori_loop(0, TOK // PAIR, project, 0)
    ring_stage(LATE, 3)

    def own_half(ref):
        return ref[pl.ds(pl.multiple_of(c * OWN, OWN), OWN), :]

    def other_half(ref):
        return ref[pl.ds(pl.multiple_of((1 - c) * OWN, OWN), OWN), :]

    def sib_copy(phase, k):
        return remote(
            to_sib.at[phase, k],
            from_sib.at[phase, k],
            sib_send.at[phase, k],
            sib_recv.at[phase, k],
            sibling,
        )

    def owner_copy(phase, k, d):
        to = (lax.rem(x + d, XC) * 2 + c, gy)
        return remote(
            to_owner.at[phase, k],
            from_peer.at[phase, k],
            sum_send.at[phase, k],
            sum_recv.at[phase, k],
            to,
        )

    def give_halves(phase, k):
        kept[phase, k] = own_half(partial)
        to_sib[phase, k] = other_half(partial).astype(BF16)
        sib_copy(phase, k).start()

    def chip_sum(phase, k):
        sib_copy(phase, k).wait_recv()
        return kept[phase, k] + from_sib[phase, k].astype(F32)

    def send_sum(phase, k, d):
        to_owner[phase, k] = chip_sum(phase, k).astype(BF16)
        owner_copy(phase, k, d).start()

    query_row = jnp.where(
        rows_of((2 * PAIR, CHUNK)) >= PAIR, rows_of((2 * PAIR, CHUNK)) - PAIR, rows_of((2 * PAIR, CHUNK))
    )
    key_col = lanes((2 * PAIR, CHUNK))

    def far_first(k):
        return jnp.where(k == 0, 2, jnp.where(k == 1, 1, jnp.where(k == 2, 3, 0)))

    def attend(k, carry):
        block = lax.rem(x + far_first(k), XC)
        at = pl.multiple_of(block * PAIR, PAIR)
        q = queries[pl.ds(at, PAIR), :]
        zero = jnp.zeros_like(q)
        both = jnp.concatenate([jnp.where(low_head, q, zero), jnp.where(low_head, zero, q)], axis=0)
        lhs = jnp.concatenate([both, jnp.ones((2 * PAIR, HQ), BF16)], axis=1)
        top = jnp.full((2 * PAIR, HQ), -jnp.inf, F32)
        for n in range(CHUNKS):
            s = dot_nt(lhs, keys[pl.ds(at + n * CHUNK, CHUNK), :])
            if n == 0:
                s = jnp.where(key_col >= query_row + FIRST, s, AWAY)
            if n == CHUNKS - 1:
                s = jnp.where(key_col + n * CHUNK <= query_row + NEW_AT, s, AWAY)
            scores[:, n * CHUNK : (n + 1) * CHUNK] = s
            top = jnp.maximum(top, jnp.maximum(s[:, 0:HQ], s[:, HQ:]))
        highest = jnp.max(top, axis=-1, keepdims=True)
        weighted = jnp.zeros((2 * PAIR, 2 * HQ), F32)
        for n in range(CHUNKS):
            w = jnp.exp(scores[:, n * CHUNK : (n + 1) * CHUNK] - highest).astype(BF16)
            weighted += dot(w, values[pl.ds(at + n * CHUNK, CHUNK), :])
        mean = weighted[:, 0:HQ] / weighted[:, HQ:]
        attended = jnp.where(low_head, mean[0:PAIR], mean[PAIR:]).astype(BF16)
        partial[...] = dot_nt(attended, g_out[...])
        give_halves(0, k)

        @pl.when(k > 0)
        def _():
            send_sum(0, k - 1, far_first(k - 1))

        return carry

    def finish(parts, step):
        for part in parts:
            for way in (0, 1):
                if last_step(part, way) == step:
                    copy, zz = ring_copy(part, way, step, True)
                    copy.wait_recv()
                    if part == 2:
                        for copy in quarter_copies(way, step, zz):
                            go(copy)

    ring_stage(LATE, 4)
    finish((4,), 4)
    lax.fori_loop(0, 4, attend, 0)
    finish((2, 3, 5), 4)

    total = chip_sum(0, 3)
    for k, d in ((0, 2), (1, 1), (2, 3)):
        owner_copy(0, k, d).wait_recv()
        total = total + from_peer[0, k].astype(F32)
    residual = tokens[block_of(gx), :].astype(F32)
    updated = rms_unit(residual + alpha_attn[...] * (rms_unit(total) - residual)).astype(BF16)
    after[block_of(gx), :] = updated
    for d in (0, 1, 3, 2):
        go(token_copy(after, 1, d))

    for n in range(7):
        back = n + 1 if n < 4 else ZC - (n - 3)
        zz = lax.rem(z + ZC - back, ZC)
        for d in (1, 2, 3):
            piece = g_ff.at[lax.rem(y + YC - d, YC), plane(zz)]
            remote(
                piece, piece, quarter_send.at[n, d - 1], quarter_recv.at[n, d - 1], along_y[d]
            ).wait_recv()

    def near_first(k):
        return jnp.where(k == 0, 0, jnp.where(k == 1, 1, jnp.where(k == 2, 3, 2)))

    def feed(k):
        block = lax.rem(x + XC - near_first(k), XC)
        rows = after[pl.ds(pl.multiple_of(block * PAIR, PAIR), PAIR), :]
        total_low = jnp.zeros((PAIR, D), F32)
        acts = []
        for b in range(5):
            both = dot(rows, g_ff[b])
            cols = slice(b * HQ, b * HQ + HQ)
            up = both[:, 0:HQ] * s_up[:, cols]
            gate = both[:, HQ:] * s_gate[:, cols]
            acts.append((up * (gate / (1.0 + jnp.exp(-gate)))).astype(BF16))
        active = jnp.concatenate(acts, axis=1)
        partial[...] = dot_nt(active, g_down[...])
        give_halves(1, k)

    def back_of(k):
        return lax.rem(XC - near_first(k), XC)

    token_from_sibling(after, 1, 0)

    def feed_step(k, carry):
        @pl.when(k == 1)
        def _():
            for d in (1, 3):
                token_pass_on_only(d)
            token_from_sibling(after, 1, 1)

        @pl.when(k == 2)
        def _():
            token_pass_on_only(2)
            token_from_sibling(after, 1, 3)

        @pl.when(k == 3)
        def _():
            token_from_sibling(after, 1, 2)

        feed(k)

        @pl.when(k >= 2)
        def _():
            send_sum(1, k - 1, back_of(k - 1))

        return carry

    def pass_on_copy(d):
        came = block_of(lax.rem(x + XC - d, XC) * 2 + c)
        return remote(
            after.at[came], after.at[came], tok_send.at[1, 3 + d], tok_recv.at[1, 3 + d], sibling
        )

    def token_pass_on_only(d):
        came = block_of(lax.rem(x + XC - d, XC) * 2 + c)
        remote(
            after.at[came], after.at[came], tok_send.at[1, d], tok_recv.at[1, d], along_x[d]
        ).wait_recv()
        pass_on_copy(d).start()

    lax.fori_loop(0, 4, feed_step, 0)
    send_sum(1, 3, 2)
    lowered = chip_sum(1, 0)
    for k in (1, 2, 3):
        owner_copy(1, k, 1).wait_recv()
        lowered = lowered + from_peer[1, k].astype(F32)
    wide = updated.astype(F32)
    result[0] = rms_unit(wide + alpha_mlp[...] * (rms_unit(lowered) - wide)).astype(BF16)

    for copy in sent:
        copy.wait_send()
    for k in range(4):
        for phase in (0, 1):
            sib_copy(phase, k).wait_send()
    for k, d in ((0, 2), (1, 1), (2, 3)):
        owner_copy(0, k, d).wait_send()
    for k, d in ((1, 3), (2, 1), (3, 2)):
        owner_copy(1, k, d).wait_send()
    for d in (1, 2, 3):
        pass_on_copy(d).wait_send()


def per_device(
    hidden,
    lengths,
    sink_kv,
    kv_cycle,
    w_qkv,
    s_qk,
    w_out,
    alpha_attn,
    w_up,
    w_gate,
    s_up,
    s_gate,
    w_down,
    alpha_mlp,
):
    sinks = jnp.concatenate([kv_cycle[0, :, TAIL : TAIL + 12], sink_kv[0]], axis=1)
    vmem = pl.BlockSpec(memory_space=pltpu.VMEM)
    anywhere = pl.BlockSpec(memory_space=pl.ANY)
    dma = pltpu.SemaphoreType.DMA
    result, fresh = pl.pallas_call(
        layer_kernel,
        out_shape=(
            jax.ShapeDtypeStruct((1, OWN, D), BF16),
            jax.ShapeDtypeStruct((1, 2, TOK, HQ), BF16),
        ),
        in_specs=[
            pl.BlockSpec(memory_space=pltpu.SMEM),
            anywhere,
            vmem,
            anywhere,
            vmem,
            vmem,
            vmem,
            vmem,
            vmem,
            vmem,
            vmem,
            vmem,
            vmem,
            vmem,
        ],
        out_specs=(vmem, vmem),
        scratch_shapes=[
            pltpu.VMEM((D, 3 * HQ), BF16),
            pltpu.VMEM((D, HQ), BF16),
            pltpu.VMEM((5, D, 2 * HQ), BF16),
            pltpu.VMEM((D, FF), BF16),
            pltpu.VMEM((YC, 16, 3 * HQ), BF16),
            pltpu.VMEM((YC, 16, HQ + 3 * FF), BF16),
            pltpu.VMEM((TOK, D), BF16),
            pltpu.VMEM((KEYS, 2 * HQ), BF16),
            pltpu.VMEM((KEYS, 2 * HQ), BF16),
            pltpu.VMEM((TOK, HQ), BF16),
            pltpu.VMEM((2 * PAIR, CHUNK * CHUNKS), F32),
            pltpu.VMEM((PAIR, D), F32),
            pltpu.VMEM((2, 4, OWN, D), F32),
            pltpu.VMEM((2, 4, OWN, D), BF16),
            pltpu.VMEM((2, 4, OWN, D), BF16),
            pltpu.VMEM((2, 4, OWN, D), BF16),
            pltpu.VMEM((2, 4, OWN, D), BF16),
            pltpu.VMEM((TOK, D), BF16),
            dma((5,)),
            dma((2, 7)),
            dma((2, 7)),
            dma((6, 3)),
            dma((6, 3)),
            dma((6, 2, 4)),
            dma((6, 2, 4)),
            dma((7, 3)),
            dma((7, 3)),
            dma((2, 4)),
            dma((2, 4)),
            dma((2, 4)),
            dma((2, 4)),
        ],
        compiler_params=pltpu.CompilerParams(
            collective_id=0, has_side_effects=True, vmem_limit_bytes=56 * 2**20
        ),
    )(
        lengths,
        hidden,
        sinks,
        kv_cycle,
        w_qkv.reshape(SHARD, 3 * HQ),
        s_qk.reshape(1, HQ),
        w_out,
        alpha_attn.reshape(1, D),
        w_up,
        w_gate,
        s_up.reshape(1, FF),
        s_gate.reshape(1, FF),
        w_down,
        alpha_mlp.reshape(1, D),
    )
    start = lax.rem(lengths[0] - SINK, CYCLE)
    new_cycle = lax.dynamic_update_slice(kv_cycle, fresh, (0, 0, start, 0))
    return result, new_cycle


def solution(mesh):
    return jax.shard_map(
        per_device,
        mesh=mesh,
        in_specs=(
            P("gy", "gx", None),
            P("gy"),
            P("gy", None, None, "gx"),
            P("gy", None, None, "gx"),
            P("gy", None, "gx"),
            P("gx"),
            P("gx", "gy"),
            P(),
            P("gy", "gx"),
            P("gy", "gx"),
            P("gx"),
            P("gx"),
            P("gx", "gy"),
            P(),
        ),
        out_specs=(P("gy", "gx", None), P("gy", None, None, "gx")),
        check_vma=False,
    )
```

time: 234 us -> 116 us (0.50)
  the two profiles are of different devices: /device:TPU:8 before, /device:TPU:1 now
where the time goes in v1:
time: 116 us
  Pallas kernels  102 us (88%)
  local copies, waits for them, and re-layouts  11.3 us (10%)
  between operations  1.4 us (1%)
    pallas_call x1, Pallas kernels, per_device(): pl.pallas_call(layer_kernel, out_shape=(jax.ShapeDtypeStruct((1, OWN, D),...  102 us
    unnamed x22, local copies, waits for them, and re-layouts  4.87 us
    dynamic_update_slice x1, local copies, waits for them, and re-layouts, per_device(): new_cycle = lax.dynamic_update_slice(kv_cycle, fresh, (0, 0, start, 0))  3.46 us

profile of v1, /device:TPU:1, one launch (start us, length us, event | category | flops | bytes accessed | tf_op | source)
XLA Modules:
  0.0 115.6 jit_solution(14297211935904602146)
XLA Ops:
  0.6 0.0 copy-start
  0.6 0.0 copy-start.8
  0.7 0.0 copy-start.3
  0.7 0.0 copy-start.4
  0.7 0.0 copy-start.6
  0.7 0.0 copy-start.7
  0.7 0.0 copy-start.2
  0.7 0.0 copy-start.5
  0.7 1.7 %copy.28.cached = bf16[1,2,4608,128]{3,2,1,0:T(8,128)(2,1)S(1)} copy(bf16[1,2,4608,128]{3,2,1,0:T(8,128)(2,1)} %param.17) | data formatting | bytes 4718592
  2.4 0.0 copy-start.1
  3.1 0.0 copy-done.8
  3.1 0.7 pad_maximum_fusion.sinks
  3.8 0.0 copy-done
  3.8 0.6 copy_bitcast_fusion.w_qkv
  4.4 0.0 copy-done.3
  4.4 0.7 copy.20.w_out
  5.1 0.0 copy-done.4
  5.1 0.6 reshape.28.alpha_attn
  5.7 0.0 copy-done.6
  5.7 0.6 reshape.29.s_up
  6.3 0.0 copy-done.7
  6.3 0.6 reshape.30.s_gate
  6.9 0.0 copy-done.2
  6.9 0.8 copy.21.w_down
  7.7 0.0 copy-done.5
  7.7 0.6 reshape.31.alpha_mlp
  8.3 0.0 copy-done.1
  8.3 102.2 %shard_map.149 = (bf16[1,64,1280]{2,1,0:T(8,128)(2,1)}, bf16[1,2,512,128]{3,2,1,0:T(8,128)(2,1)}) custom-call(s32[1]{0:T(128)S(6)} %copy.27.lengths, bf16[1,64,1280]{2,1,0:T(8,128)(2,1)} %hidden.1, bf16[2,16,128]{2,1,0:T(8,128)(2,1)} %pad_maximum_fusion.sinks, bf16[1,2,4608,128]{3,2,1,0:T(8,128)(2,1)} %copy-done.1, bf16[40,384]{1,0:T(8,128)(2,1)} %copy_bitcast_fusion.w_qkv, ...), custom_call_target="tpu_custom_call" | custom-call | tf_op jit(solution)/shard_map/pallas_call | solution.py:612
  110.6 3.5 %dynamic_update_slice.3 = bf16[1,2,4608,128]{3,2,1,0:T(8,128)(2,1)} dynamic-update-slice(bf16[1,2,4608,128]{3,2,1,0:T(8,128)(2,1)} %copy-done.1, bf16[1,2,512,128]{3,2,1,0:T(8,128)(2,1)} %get-tuple-element.5, s32[]{:T(128)} %constant.6.clone.1, s32[]{:T(128)} %constant.6.clone.1, s32[]{:T(128)S(6)} %select_n.3, s32[]{:T(128)} %constant.6.clone.1) | dynamic-update-slice | bytes 524292 | tf_op jit(solution)/shard_map/dynamic_update_slice | solution.py:688
  114.0 1.6 %copy.29 = bf16[1,64,1280]{2,1,0:T(8,128)(2,1)} copy(bf16[1,64,1280]{2,1,0:T(8,128)(2,1)} %get-tuple-element.8) | data formatting | bytes 327680
  (1 shorter events, 0.0 us)
Async XLA Ops:
  0.6 3.2 %copy-start = (bf16[40,3,128]{2,0,1:T(8,128)(2,1)S(1)}, bf16[40,3,128]{2,0,1:T(8,128)(2,1)}, u32[]{:S(2)}) copy-start(bf16[40,3,128]{2,0,1:T(8,128)(2,1)} %param.18) | copy-start | bytes 92164
  0.6 2.5 %copy-start.8 = (bf16[1,2,4,128]{3,2,1,0:T(4,128)(2,1)S(1)}, bf16[1,2,4,128]{3,2,1,0:T(4,128)(2,1)}, u32[]{:S(2)}) copy-start(bf16[1,2,4,128]{3,2,1,0:T(4,128)(2,1)} %param.16) | copy-start | bytes 6148
  0.7 3.7 %copy-start.3 = (bf16[128,40]{0,1:T(8,128)(2,1)S(1)}, bf16[128,40]{0,1:T(8,128)(2,1)}, u32[]{:S(2)}) copy-start(bf16[128,40]{0,1:T(8,128)(2,1)} %param.20) | copy-start | bytes 30724
  0.7 4.4 %copy-start.4 = (f32[1280]{0:T(1024)S(1)}, f32[1280]{0:T(1024)}, u32[]{:S(2)}) copy-start(f32[1280]{0:T(1024)} %param.21) | copy-start | bytes 15364
  0.7 5.0 %copy-start.6 = (f32[640]{0:T(1024)S(1)}, f32[640]{0:T(1024)}, u32[]{:S(2)}) copy-start(f32[640]{0:T(1024)} %param.24) | copy-start | bytes 7684
  0.7 5.6 %copy-start.7 = (f32[640]{0:T(1024)S(1)}, f32[640]{0:T(1024)}, u32[]{:S(2)}) copy-start(f32[640]{0:T(1024)} %param.25) | copy-start | bytes 7684
  0.7 6.2 %copy-start.2 = (bf16[640,40]{0,1:T(8,128)(2,1)S(1)}, bf16[640,40]{0,1:T(8,128)(2,1)}, u32[]{:S(2)}) copy-start(bf16[640,40]{0,1:T(8,128)(2,1)} %param.26) | copy-start | bytes 153604
  0.7 7.0 %copy-start.5 = (f32[1280]{0:T(1024)S(1)}, f32[1280]{0:T(1024)}, u32[]{:S(2)}) copy-start(f32[1280]{0:T(1024)} %param.27) | copy-start | bytes 15364
  2.4 5.9 %copy-start.1 = (bf16[1,2,4608,128]{3,2,1,0:T(8,128)(2,1)}, bf16[1,2,4608,128]{3,2,1,0:T(8,128)(2,1)S(1)}, u32[]{:S(2)}) copy-start(bf16[1,2,4608,128]{3,2,1,0:T(8,128)(2,1)S(1)} %copy.28.cached) | copy-start | bytes 7077892

commit v2 on v1

v2 whole, which is shorter than its diff:
```python
import functools

import jax
import jax.numpy as jnp
from jax import lax
from jax.experimental import pallas as pl
from jax.experimental.pallas import tpu as pltpu
from jax.sharding import PartitionSpec as P

MESH = pl.DeviceIdType.MESH
BF16 = jnp.bfloat16
F32 = jnp.float32

XC, YC, ZC = 4, 4, 8
D = 1280
HQ = 128
FF = 640
TOK = 512
OWN = 64
PAIR = 128
SHARD = 40
PLANE = SHARD * YC
SINK = 4
WINDOW = 4096
CYCLE = 4608
LONG = 16384
HEAD = 3056
TAIL = 2544
OLD = CYCLE - HEAD + TAIL
NEW_AT = OLD + 16
CHUNK = 256
CHUNKS = 17
KEYS = 3 * PAIR + CHUNK * CHUNKS
FIRST = 13
AWAY = -1e30
DOWN, REST, FRONT = 0, 1, 2
OUT = 2
GATE_FRONT = 256
GATE_REST = FF - GATE_FRONT
RIGHT_LAST = (DOWN,)


def dot(a, b):
    return jnp.dot(a, b, preferred_element_type=F32)


def dot_nt(a, b):
    return lax.dot_general(a, b, (((1,), (1,)), ((), ())), preferred_element_type=F32)


def rms_unit(values):
    return values * lax.rsqrt(jnp.mean(values * values, axis=-1, keepdims=True) + 1e-06)


def lanes(shape):
    return lax.broadcasted_iota(jnp.int32, shape, len(shape) - 1)


def rows_of(shape):
    return lax.broadcasted_iota(jnp.int32, shape, len(shape) - 2)


def layer_kernel(
    lengths,
    hidden,
    sinks,
    cached,
    w_qkv,
    s_qk,
    w_out,
    alpha_attn,
    w_up,
    w_gate,
    s_up,
    s_gate,
    w_down,
    alpha_mlp,
    result,
    fresh,
    l_qkv,
    l_out,
    l_down,
    l_rest,
    l_front,
    g_qkv,
    g_out,
    g_ff,
    g_down,
    tokens,
    keys,
    values,
    queries,
    even_scores,
    odd_scores,
    attended,
    partial,
    kept,
    to_sib,
    from_sib,
    to_owner,
    from_peer,
    after,
    local_sem,
    tok_send,
    tok_recv,
    qkv_send,
    qkv_recv,
    out_send,
    out_recv,
    shard_send,
    shard_recv,
    ring_send,
    ring_recv,
    quarter_send,
    quarter_recv,
    sib_send,
    sib_recv,
    sum_send,
    sum_recv,
):
    gx = lax.axis_index("gx")
    gy = lax.axis_index("gy")
    x, c = gx // 2, lax.rem(gx, 2)
    z, y = gy // YC, lax.rem(gy, YC)

    def device(dx=0, other=False, dz=0, dy=0):
        core = 1 - c if other else c
        return (
            lax.rem(x + dx, XC) * 2 + core,
            lax.rem(z + dz, ZC) * YC + lax.rem(y + dy, YC),
        )

    sibling = device(other=True)
    along_x = {d: device(dx=d) for d in (1, 2, 3)}
    along_y = {d: device(dy=d) for d in (1, 2, 3)}
    right, left = device(dz=1), device(dz=ZC - 1)
    along_z = [device(dz=d) for d in range(1, ZC)]
    everyone = [sibling, *along_x.values(), *along_y.values(), *along_z]
    gate_sem = pltpu.get_barrier_semaphore()
    for peer in everyone:
        pl.semaphore_signal(gate_sem, inc=1, device_id=peer, device_id_type=MESH)

    sent = []

    def remote(src, dst, send, recv, to):
        return pltpu.make_async_remote_copy(
            src_ref=src, dst_ref=dst, send_sem=send, recv_sem=recv, device_id=to, device_id_type=MESH
        )

    def go(copy):
        copy.start()
        sent.append(copy)

    def block_of(g):
        return pl.ds(pl.multiple_of(g * OWN, OWN), OWN)

    own_in = pltpu.make_async_copy(hidden.at[0], tokens.at[block_of(gx)], local_sem.at[0])
    own_in.start()
    loads = []
    for kind, store in ((0, keys), (1, values)):
        for n, (src, at, count) in enumerate(
            ((HEAD, 0, CYCLE - HEAD), (0, CYCLE - HEAD, TAIL + 16))
        ):
            loads.append(
                pltpu.make_async_copy(
                    cached.at[0, kind, pl.ds(src, count)],
                    store.at[pl.ds(at, count), pl.ds(0, HQ)],
                    local_sem.at[1 + 2 * kind + n],
                )
            )
    for load in loads:
        load.start()

    mine = [
        (w_qkv, l_qkv.at[z, y]),
        (w_up, l_front.at[z, y, :, pl.ds(0, FF)]),
        (w_gate.at[:, pl.ds(0, GATE_FRONT)], l_front.at[z, y, :, pl.ds(FF, GATE_FRONT)]),
        (w_gate.at[:, pl.ds(GATE_FRONT, GATE_REST)], l_rest.at[z, y, :, pl.ds(0, GATE_REST)]),
        (w_down, l_down.at[z, y]),
        (w_out, l_out.at[z, y]),
    ]
    mine = [pltpu.make_async_copy(a, b, local_sem.at[5 + n]) for n, (a, b) in enumerate(mine)]
    for copy in mine:
        copy.start()

    def over_y(piece, sends, recvs):
        return [remote(piece, piece, sends(d - 1), recvs(d - 1), along_y[d]) for d in (1, 2, 3)]

    def qkv_over_z(dz, arriving=False):
        zz = lax.rem(z + ZC - dz, ZC) if arriving else z
        piece = l_qkv.at[zz, y]
        return remote(piece, piece, qkv_send.at[0, dz], qkv_recv.at[0, dz], device(dz=dz))

    def qkv_over_y(dz):
        piece = l_qkv.at[lax.rem(z + ZC - dz, ZC), y]
        return over_y(piece, lambda n: qkv_send.at[1 + n, dz], lambda n: qkv_recv.at[1 + n, dz])

    def out_over_z(dz, arriving=False):
        piece = l_out.at[lax.rem(z + ZC - dz, ZC) if arriving else z]
        return remote(piece, piece, out_send.at[dz], out_recv.at[dz], device(dz=dz))

    def from_y(d):
        return lax.rem(y + YC - d, YC)

    def shard_over_y(part):
        piece = (l_down, l_rest, l_out)[part].at[z, y]
        return over_y(piece, lambda n: shard_send.at[part, n], lambda n: shard_recv.at[part, n])

    def shard_arrived(part):
        for d in (1, 2, 3):
            piece = (l_down, l_rest, l_out)[part].at[z, from_y(d)]
            remote(
                piece, piece, shard_send.at[part, d - 1], shard_recv.at[part, d - 1], along_y[d]
            ).wait_recv()

    def last_step(part, way):
        return 4 if (part in RIGHT_LAST) == (way == 0) else 3

    def ring_copy(part, way, step, arriving):
        back = step if arriving else step - 1
        zz = lax.rem(z + ZC - back, ZC) if way == 0 else lax.rem(z + back, ZC)
        piece = (l_down.at[zz], l_rest.at[zz], l_front.at[zz, y])[part]
        return remote(
            piece,
            piece,
            ring_send.at[part, way, step - 1],
            ring_recv.at[part, way, step - 1],
            right if way == 0 else left,
        )

    def front_over_y(n):
        piece = l_front.at[lax.rem(z + ZC - n, ZC), y]
        return over_y(piece, lambda m: quarter_send.at[n, m], lambda m: quarter_recv.at[n, m])

    def ring_stage(part, step):
        for way in (0, 1):
            if 1 <= step - 1 <= last_step(part, way):
                ring_copy(part, way, step - 1, True).wait_recv()
            if step <= last_step(part, way):
                go(ring_copy(part, way, step, False))

    pl.semaphore_wait(gate_sem, len(everyone))
    mine[0].wait()
    for dz in (1, 7, 2, 6, 3, 5, 4):
        go(qkv_over_z(dz))
    mine[5].wait()
    for copy in (*shard_over_y(OUT), *qkv_over_y(0)):
        go(copy)
    for n in (3, 4):
        mine[n].wait()
    for part in (DOWN, REST):
        for copy in shard_over_y(part):
            go(copy)

    own_in.wait()

    def held_by(d, other=False):
        core = 1 - c if other else c
        return lax.rem(x + XC - d, XC) * 2 + core

    def token_piece(g):
        return tokens.at[block_of(g)]

    def out_piece(g):
        return g_out.at[g]

    def attended_piece(n):
        return lambda g: attended.at[g, pl.ds(pl.multiple_of(n * PAIR, PAIR), PAIR)]

    def x_copy(piece, phase, d):
        to = sibling if d == 0 else along_x[d]
        return remote(piece(gx), piece(gx), tok_send.at[phase, d], tok_recv.at[phase, d], to)

    def x_pass_copy(piece, phase, d):
        block = piece(held_by(d))
        return remote(block, block, tok_send.at[phase, 3 + d], tok_recv.at[phase, 3 + d], sibling)

    def x_pass_on(piece, phase, d):
        block = piece(held_by(d))
        remote(
            block, block, tok_send.at[phase, d], tok_recv.at[phase, d], along_x[d]
        ).wait_recv()
        go(x_pass_copy(piece, phase, d))

    def x_from_sibling(piece, phase, d):
        block = piece(held_by(d, True))
        n = 0 if d == 0 else 3 + d
        remote(block, block, tok_send.at[phase, n], tok_recv.at[phase, n], sibling).wait_recv()

    for d in (1, 3, 2, 0):
        go(x_copy(token_piece, 0, d))

    for n in (1, 2):
        mine[n].wait()
    ring_stage(FRONT, 1)

    def pass_on_qkv(dz):
        qkv_over_z(dz, True).wait_recv()
        for copy in qkv_over_y(dz):
            go(copy)

    for dz in (1, 7, 2, 6):
        pass_on_qkv(dz)
    shard_arrived(OUT)
    for dz in (1, 7, 2, 6, 3, 5, 4):
        go(out_over_z(dz))
    for dz in (3, 5, 4):
        pass_on_qkv(dz)
    for part in (DOWN, REST):
        shard_arrived(part)
        ring_stage(part, 1)

    length = lengths[0]

    def key_bias(n, carry):
        at = pl.multiple_of(n * PAIR, PAIR)
        row = rows_of((PAIR, HQ)) + at
        slot = jnp.where(row < CYCLE - HEAD, row + HEAD, row - (CYCLE - HEAD))
        lag = length - 1 - SINK - slot
        turns = (
            jnp.where(lag >= CYCLE, 1, 0)
            + jnp.where(lag >= 2 * CYCLE, 1, 0)
            + jnp.where(lag >= 3 * CYCLE, 1, 0)
        )
        held = SINK + slot + CYCLE * turns
        old = (lag >= 0) & (held >= length - WINDOW) & (row < OLD + 12)
        seen = old | ((row >= OLD + 12) & (row < NEW_AT + TOK))
        keys[pl.ds(at, PAIR), HQ : 2 * HQ] = jnp.where(seen, 0.0, AWAY).astype(BF16)
        values[pl.ds(at, PAIR), HQ : 2 * HQ] = jnp.ones((PAIR, HQ), BF16)
        return carry

    lax.fori_loop(0, KEYS // PAIR, key_bias, 0)
    spare = KEYS - NEW_AT - TOK
    for load in loads:
        load.wait()
    tile_row = rows_of((16, HQ))
    for kind, store in ((0, keys), (1, values)):
        store[NEW_AT + TOK :, 0:HQ] = jnp.zeros((spare, HQ), BF16)
        tile = store[OLD:NEW_AT, 0:HQ].astype(F32)
        sink_rows = sinks[0, kind].astype(F32)
        for r in range(SINK):
            tile = jnp.where(tile_row == 12 + r, sink_rows[r : r + 1], tile)
        store[OLD:NEW_AT, 0:HQ] = tile.astype(BF16)

    for d in (1, 3, 2):
        x_pass_on(token_piece, 0, d)

    def assemble(p, take, put):
        zz, pair = p // 2, lax.rem(p, 2)
        low, high = take(zz, 2 * pair), take(zz, 2 * pair + 1)
        put(
            pl.ds(pl.multiple_of(p * 2 * SHARD, 16), 2 * SHARD),
            jnp.concatenate([low.astype(F32), high.astype(F32)], axis=0).astype(BF16),
        )

    def put_out(rows, value):
        g_out[gx, rows, :] = value

    def assemble_out(p, carry):
        assemble(p, lambda zz, yy: l_out[zz, yy], put_out)
        return carry

    for dz in (1, 7, 2, 6, 3, 5, 4):
        out_over_z(dz, True).wait_recv()
    lax.fori_loop(0, D // (2 * SHARD), assemble_out, 0)
    for d in (2, 1, 3, 0):
        go(x_copy(out_piece, 1, d))
    ring_stage(FRONT, 2)
    for n in range(ZC):
        for d in (1, 2, 3):
            piece = l_qkv.at[lax.rem(z + ZC - n, ZC), from_y(d)]
            remote(
                piece, piece, qkv_send.at[d, n], qkv_recv.at[d, n], along_y[d]
            ).wait_recv()
    for n in (0, 1, 7):
        for copy in front_over_y(n):
            go(copy)

    def assemble_qkv(p, carry):
        for n in range(3):

            def put(rows, value, n=n):
                g_qkv[rows, n * HQ : (n + 1) * HQ] = value

            assemble(p, lambda zz, yy, n=n: l_qkv[zz, yy, n], put)
        return carry

    lax.fori_loop(0, D // (2 * SHARD), assemble_qkv, 0)
    for d in (0, 1, 2, 3):
        x_from_sibling(token_piece, 0, d)

    low_head = lanes((PAIR, HQ)) < 64

    def head_unit(v):
        squares = v * v
        low = jnp.sum(jnp.where(low_head, squares, 0.0), axis=-1, keepdims=True)
        high = jnp.sum(jnp.where(low_head, 0.0, squares), axis=-1, keepdims=True)
        return v * jnp.where(low_head, lax.rsqrt(low + 1e-06), lax.rsqrt(high + 1e-06))

    def project(n, carry):
        at = pl.multiple_of(n * PAIR, PAIR)
        qkv = dot(tokens[pl.ds(at, PAIR), :], g_qkv[...])
        scale = s_qk[...]
        q = (head_unit(qkv[:, 0:HQ]) * scale).astype(BF16)
        queries[pl.ds(at, PAIR), :] = (q.astype(F32) * 8.0).astype(BF16)
        k = (head_unit(qkv[:, HQ : 2 * HQ]) * scale).astype(BF16)
        v = qkv[:, 2 * HQ :].astype(BF16)
        to = pl.ds(pl.multiple_of(NEW_AT + at, 16), PAIR)
        keys[to, 0:HQ] = k
        values[to, 0:HQ] = v
        fresh[0, 0, pl.ds(at, PAIR), :] = k
        fresh[0, 1, pl.ds(at, PAIR), :] = v
        return carry

    lax.fori_loop(0, TOK // PAIR, project, 0)
    ring_stage(DOWN, 2)
    ring_stage(REST, 2)
    ring_stage(FRONT, 3)
    for n in (2, 6):
        for copy in front_over_y(n):
            go(copy)

    def own_half(ref):
        return ref[pl.ds(pl.multiple_of(c * OWN, OWN), OWN), :]

    def other_half(ref):
        return ref[pl.ds(pl.multiple_of((1 - c) * OWN, OWN), OWN), :]

    def sib_copy(k):
        return remote(
            to_sib.at[k],
            from_sib.at[k],
            sib_send.at[k],
            sib_recv.at[k],
            sibling,
        )

    def owner_copy(k, d):
        to = (lax.rem(x + d, XC) * 2 + c, gy)
        return remote(
            to_owner.at[k],
            from_peer.at[k],
            sum_send.at[k],
            sum_recv.at[k],
            to,
        )

    def give_halves(k):
        kept[k] = own_half(partial)
        to_sib[k] = other_half(partial).astype(BF16)
        sib_copy(k).start()

    def chip_sum(k):
        sib_copy(k).wait_recv()
        return kept[k] + from_sib[k].astype(F32)

    def send_sum(k, d):
        to_owner[k] = chip_sum(k).astype(BF16)
        owner_copy(k, d).start()

    query_row = jnp.where(
        rows_of((2 * PAIR, CHUNK)) >= PAIR, rows_of((2 * PAIR, CHUNK)) - PAIR, rows_of((2 * PAIR, CHUNK))
    )
    key_col = lanes((2 * PAIR, CHUNK))

    def left_side(k):
        q = queries[k * PAIR : (k + 1) * PAIR, :]
        zero = jnp.zeros_like(q)
        both = jnp.concatenate([jnp.where(low_head, q, zero), jnp.where(low_head, zero, q)], axis=0)
        return jnp.concatenate([both, jnp.ones((2 * PAIR, HQ), BF16)], axis=1)

    def score(k, n, lhs, top):
        s = dot_nt(lhs, keys[k * PAIR + n * CHUNK : k * PAIR + (n + 1) * CHUNK, :])
        if n == 0:
            s = jnp.where(key_col >= query_row + FIRST, s, AWAY)
        if n == CHUNKS - 1:
            s = jnp.where(key_col + n * CHUNK <= query_row + NEW_AT, s, AWAY)
        (even_scores, odd_scores)[k % 2][:, n * CHUNK : (n + 1) * CHUNK] = s
        part = jnp.maximum(s[:, 0:HQ], s[:, HQ:])
        return part if top is None else jnp.maximum(top, part)

    def weigh(k, n, highest, weighted):
        s = (even_scores, odd_scores)[k % 2][:, n * CHUNK : (n + 1) * CHUNK]
        w = jnp.exp(s - highest).astype(BF16)
        part = dot(w, values[k * PAIR + n * CHUNK : k * PAIR + (n + 1) * CHUNK, :])
        return part if weighted is None else weighted + part

    def attend():
        highest = None
        for k in range(5):
            if k == 2:
                ring_stage(FRONT, 4)
                for n in (3, 5):
                    for copy in front_over_y(n):
                        go(copy)
            if k == 4:
                ring_stage(DOWN, 3)
                ring_stage(REST, 3)
            top, weighted = None, None
            lhs = left_side(k) if k < 4 else None
            for n in range(CHUNKS):
                if k > 0:
                    weighted = weigh(k - 1, n, highest, weighted)
                if k < 4:
                    top = score(k, n, lhs, top)
            if k > 0:
                mean = weighted[:, 0:HQ] / weighted[:, HQ:]
                attended[gx, (k - 1) * PAIR : k * PAIR, :] = jnp.where(
                    low_head, mean[0:PAIR], mean[PAIR:]
                ).astype(BF16)
                for d in range(XC):
                    go(x_copy(attended_piece(k - 1), 1 + k, d))
            if k < 4:
                highest = jnp.max(top, axis=-1, keepdims=True)

    def finish(part):
        for way in (0, 1):
            if last_step(part, way) == 4:
                ring_copy(part, way, 4, True).wait_recv()

    attend()
    finish(FRONT)
    for copy in front_over_y(4):
        go(copy)
    for d in (1, 3, 2):
        x_pass_on(out_piece, 1, d)
    for n in range(3):
        for d in (1, 3, 2):
            x_pass_on(attended_piece(n), 2 + n, d)

    def wide_row(ref, count):
        return jnp.concatenate([ref[n : n + 1, :] for n in range(count)], axis=1)

    alpha_a = wide_row(alpha_attn, D // HQ)

    def update(k, carry):
        rows = slice(k * PAIR, (k + 1) * PAIR)
        heads = jnp.concatenate([attended[g, rows, :] for g in range(2 * XC)], axis=1)
        out = jnp.concatenate([g_out[g] for g in range(2 * XC)], axis=1)
        mixed = dot_nt(heads, out)
        residual = tokens[rows, :].astype(F32)
        after[rows, :] = rms_unit(residual + alpha_a * (rms_unit(mixed) - residual)).astype(BF16)
        return carry

    for d in range(XC):
        x_from_sibling(out_piece, 1, d)
    for n in range(4):
        for d in range(XC):
            x_from_sibling(attended_piece(n), 2 + n, d)
        update(n, 0)
        if n == 0:
            for d in (1, 3, 2):
                x_pass_on(attended_piece(3), 5, d)
    ring_stage(DOWN, 4)
    ring_stage(REST, 4)

    for n in range(ZC):
        for d in (1, 2, 3):
            piece = l_front.at[lax.rem(z + ZC - n, ZC), from_y(d)]
            remote(
                piece, piece, quarter_send.at[n, d - 1], quarter_recv.at[n, d - 1], along_y[d]
            ).wait_recv()

    def gate_block(b):
        at = b * HQ
        if at < GATE_FRONT:
            return lambda zz, yy: l_front[zz, yy, :, FF + at : FF + at + HQ]
        at -= GATE_FRONT
        return lambda zz, yy: l_rest[zz, yy, :, at : at + HQ]

    def assemble_ff(p, carry):
        for b in range(FF // HQ):

            def put_up(rows, value, b=b):
                g_ff[b, rows, 0:HQ] = value

            def put_gate(rows, value, b=b):
                g_ff[b, rows, HQ : 2 * HQ] = value

            assemble(p, lambda zz, yy, b=b: l_front[zz, yy, :, b * HQ : (b + 1) * HQ], put_up)
            assemble(p, gate_block(b), put_gate)

        def put_down(rows, value):
            g_down[rows, :] = value

        assemble(p, lambda zz, yy: l_down[zz, yy], put_down)
        return carry

    finish(DOWN)
    finish(REST)
    lax.fori_loop(0, D // (2 * SHARD), assemble_ff, 0)

    s_up_row = wide_row(s_up, FF // HQ)
    s_gate_row = wide_row(s_gate, FF // HQ)

    def far_first(k):
        return jnp.where(k == 0, 2, jnp.where(k == 1, 1, jnp.where(k == 2, 3, 0)))

    def feed(k):
        block = lax.rem(x + far_first(k), XC)
        rows = after[pl.ds(pl.multiple_of(block * PAIR, PAIR), PAIR), :]
        acts = []
        for b in range(5):
            both = dot(rows, g_ff[b])
            cols = slice(b * HQ, b * HQ + HQ)
            up = both[:, 0:HQ] * s_up_row[:, cols]
            gate = both[:, HQ:] * s_gate_row[:, cols]
            acts.append((up * (gate / (1.0 + jnp.exp(-gate)))).astype(BF16))
        active = jnp.concatenate(acts, axis=1)
        partial[...] = dot_nt(active, g_down[...])
        give_halves(k)

    def feed_step(k, carry):
        feed(k)

        @pl.when(k >= 1)
        def _():
            send_sum(k - 1, far_first(k - 1))

        return carry

    lax.fori_loop(0, 4, feed_step, 0)
    lowered = chip_sum(3)
    for k, d in ((0, 2), (1, 1), (2, 3)):
        owner_copy(k, d).wait_recv()
        lowered = lowered + from_peer[k].astype(F32)
    wide = after[block_of(gx), :].astype(F32)
    alpha_m = wide_row(alpha_mlp, D // HQ)
    result[0] = rms_unit(wide + alpha_m * (rms_unit(lowered) - wide)).astype(BF16)

    for copy in sent:
        copy.wait_send()
    for k in range(4):
        sib_copy(k).wait_send()
    for k, d in ((0, 2), (1, 1), (2, 3)):
        owner_copy(k, d).wait_send()


SPAN = TOK + 16


BANDS = 4


def append_kernel(
    lengths, cached, fresh, hidden, new_hidden, new_cycle, cycle, new_rows, own, sem
):
    start = jnp.clip(lax.rem(lengths[0] - SINK, CYCLE), 0, CYCLE - SPAN)
    base = pl.multiple_of(start // 16 * 16, 16)
    shift = start - base
    bands = [(n, b, pl.ds(b * (CYCLE // BANDS), CYCLE // BANDS)) for n in (0, 1) for b in range(BANDS)]
    loads = [pltpu.make_async_copy(cached.at[0, n, r], cycle.at[n, r], sem.at[0, n, b]) for n, b, r in bands]
    stores = [pltpu.make_async_copy(cycle.at[n, r], new_cycle.at[0, n, r], sem.at[1, n, b]) for n, b, r in bands]
    rows_in = pltpu.make_async_copy(fresh.at[0], new_rows, sem.at[2, 0, 0])
    own_in = pltpu.make_async_copy(hidden.at[0], own, sem.at[2, 0, 1])
    own_out = pltpu.make_async_copy(own, new_hidden.at[0], sem.at[2, 0, 2])
    for load in (rows_in, own_in, *loads):
        load.start()
    row = rows_of((SPAN, HQ))
    here = (row >= shift) & (row < shift + TOK)
    rows_in.wait()
    for n in (0, 1):
        rows = jnp.concatenate([new_rows[n].astype(F32), jnp.zeros((16, HQ), F32)], axis=0)
        rows = pltpu.roll(rows, shift, 0)
        if n == 0:
            own_in.wait()
            own_out.start()
        for load in loads[n * BANDS : (n + 1) * BANDS]:
            load.wait()
        window = cycle.at[n, pl.ds(base, SPAN)]
        window[...] = jnp.where(here, rows, window[...].astype(F32)).astype(BF16)
        for store in stores[n * BANDS : (n + 1) * BANDS]:
            store.start()
    for copy in (*stores, own_out):
        copy.wait()


def per_device(
    hidden,
    lengths,
    sink_kv,
    kv_cycle,
    w_qkv,
    s_qk,
    w_out,
    alpha_attn,
    w_up,
    w_gate,
    s_up,
    s_gate,
    w_down,
    alpha_mlp,
):
    vmem = pl.BlockSpec(memory_space=pltpu.VMEM)
    anywhere = pl.BlockSpec(memory_space=pl.ANY)
    dma = pltpu.SemaphoreType.DMA
    result, fresh = pl.pallas_call(
        layer_kernel,
        out_shape=(
            jax.ShapeDtypeStruct((1, OWN, D), BF16),
            jax.ShapeDtypeStruct((1, 2, TOK, HQ), BF16),
        ),
        in_specs=[
            pl.BlockSpec(memory_space=pltpu.SMEM),
            anywhere,
            vmem,
            anywhere,
            anywhere,
            vmem,
            anywhere,
            vmem,
            anywhere,
            anywhere,
            vmem,
            vmem,
            anywhere,
            vmem,
        ],
        out_specs=(vmem, vmem),
        scratch_shapes=[
            pltpu.VMEM((ZC, YC, 3, SHARD, HQ), BF16),
            pltpu.VMEM((ZC, YC, SHARD, HQ), BF16),
            pltpu.VMEM((ZC, YC, SHARD, FF), BF16),
            pltpu.VMEM((ZC, YC, SHARD, GATE_REST), BF16),
            pltpu.VMEM((ZC, YC, SHARD, FF + GATE_FRONT), BF16),
            pltpu.VMEM((D, 3 * HQ), BF16),
            pltpu.VMEM((2 * XC, D, HQ), BF16),
            pltpu.VMEM((5, D, 2 * HQ), BF16),
            pltpu.VMEM((D, FF), BF16),
            pltpu.VMEM((TOK, D), BF16),
            pltpu.VMEM((KEYS, 2 * HQ), BF16),
            pltpu.VMEM((KEYS, 2 * HQ), BF16),
            pltpu.VMEM((TOK, HQ), BF16),
            pltpu.VMEM((2 * PAIR, CHUNK * CHUNKS), F32),
            pltpu.VMEM((2 * PAIR, CHUNK * CHUNKS), F32),
            pltpu.VMEM((2 * XC, TOK, HQ), BF16),
            pltpu.VMEM((PAIR, D), F32),
            pltpu.VMEM((4, OWN, D), F32),
            pltpu.VMEM((4, OWN, D), BF16),
            pltpu.VMEM((4, OWN, D), BF16),
            pltpu.VMEM((4, OWN, D), BF16),
            pltpu.VMEM((4, OWN, D), BF16),
            pltpu.VMEM((TOK, D), BF16),
            dma((11,)),
            dma((6, 7)),
            dma((6, 7)),
            dma((4, ZC)),
            dma((4, ZC)),
            dma((ZC,)),
            dma((ZC,)),
            dma((3, 3)),
            dma((3, 3)),
            dma((3, 2, 4)),
            dma((3, 2, 4)),
            dma((ZC, 3)),
            dma((ZC, 3)),
            dma((4,)),
            dma((4,)),
            dma((4,)),
            dma((4,)),
        ],
        compiler_params=pltpu.CompilerParams(
            collective_id=0, has_side_effects=True, vmem_limit_bytes=56 * 2**20
        ),
    )(
        lengths,
        hidden,
        sink_kv,
        kv_cycle,
        w_qkv.transpose(1, 0, 2),
        s_qk.reshape(1, HQ),
        w_out.T,
        alpha_attn.reshape(D // HQ, HQ),
        w_up,
        w_gate,
        s_up.reshape(FF // HQ, HQ),
        s_gate.reshape(FF // HQ, HQ),
        w_down.T,
        alpha_mlp.reshape(D // HQ, HQ),
    )
    return pl.pallas_call(
        append_kernel,
        out_shape=(
            jax.ShapeDtypeStruct((1, OWN, D), BF16),
            jax.ShapeDtypeStruct(kv_cycle.shape, BF16),
        ),
        in_specs=[pl.BlockSpec(memory_space=pltpu.SMEM), anywhere, anywhere, anywhere],
        out_specs=(anywhere, anywhere),
        scratch_shapes=[
            pltpu.VMEM((2, CYCLE, HQ), BF16),
            pltpu.VMEM((2, TOK, HQ), BF16),
            pltpu.VMEM((OWN, D), BF16),
            dma((3, 2, BANDS)),
        ],
        compiler_params=pltpu.CompilerParams(vmem_limit_bytes=56 * 2**20),
    )(lengths, kv_cycle, fresh, result)


def solution(mesh):
    return jax.shard_map(
        per_device,
        mesh=mesh,
        in_specs=(
            P("gy", "gx", None),
            P("gy"),
            P("gy", None, None, "gx"),
            P("gy", None, None, "gx"),
            P("gy", None, "gx"),
            P("gx"),
            P("gx", "gy"),
            P(),
            P("gy", "gx"),
            P("gy", "gx"),
            P("gx"),
            P("gx"),
            P("gx", "gy"),
            P(),
        ),
        out_specs=(P("gy", "gx", None), P("gy", None, None, "gx")),
        check_vma=False,
    )
```

time: 116 us -> 85.1 us (0.73)
  Pallas kernels: 102 us -> 83.7 us
  local copies, waits for them, and re-layouts: 11.3 us -> 0 us
    pallas_call x1, Pallas kernels: 102 us -> 80.4 us  [per_device(): pl.pallas_call(layer_kernel, out_shape=(jax.ShapeDtypeStruct((1, OWN, D),...]
    unnamed x22 -> x0, local copies, waits for them, and re-layouts: 4.87 us -> none
    dynamic_update_slice x1 -> x0, local copies, waits for them, and re-layouts: 3.46 us -> none  [per_device(): new_cycle = lax.dynamic_update_slice(kv_cycle, fresh, (0, 0, start, 0))]
    pallas_call x0 -> x1, Pallas kernels: none -> 3.26 us  [per_device(): pl.pallas_call(append_kernel, out_shape=(jax.ShapeDtypeStruct((1, OWN, D)...]
    reshape x5 -> x0, local copies, waits for them, and re-layouts: 2.96 us -> none  [the longest x1 0.61 us: per_device(): w_qkv.reshape(SHARD, 3 * HQ)]
where the time goes in v2:
time: 85.1 us; the launch traced here: 85 us
  Pallas kernels  83.7 us (98%)
  between operations  1.29 us (2%)
    pallas_call x1, Pallas kernels, per_device(): pl.pallas_call(layer_kernel, out_shape=(jax.ShapeDtypeStruct((1, OWN, D),...  80.4 us
    pallas_call x1, Pallas kernels, per_device(): pl.pallas_call(append_kernel, out_shape=(jax.ShapeDtypeStruct((1, OWN, D)...  3.26 us

profile of v2, /device:TPU:1, one launch (start us, length us, event | category | flops | bytes accessed | tf_op | source)
XLA Modules:
  0.0 85.0 jit_solution(9832025740032719191)
XLA Ops:
  1.3 80.4 %shard_map.149 = (bf16[1,64,1280]{2,1,0:T(8,128)(2,1)}, bf16[1,2,512,128]{3,2,1,0:T(8,128)(2,1)}) custom-call(s32[1]{0:T(128)S(6)} %copy.16.lengths, bf16[1,64,1280]{2,1,0:T(8,128)(2,1)} %hidden.1, bf16[1,2,4,128]{3,2,1,0:T(4,128)(2,1)} %sinks.1, bf16[1,2,4608,128]{3,2,1,0:T(8,128)(2,1)} %cached.3, bf16[3,40,128]{2,1,0:T(8,128)(2,1)} %bitcast.9, ...), custom_call_target="tpu_custom_call" | custom-call | tf_op jit(solution)/shard_map/pallas_call | solution.py:697
  81.7 3.3 %shard_map.150 = (bf16[1,64,1280]{2,1,0:T(8,128)(2,1)}, bf16[1,2,4608,128]{3,2,1,0:T(8,128)(2,1)}) custom-call(s32[1]{0:T(128)S(6)} %copy.16.lengths, bf16[1,2,4608,128]{3,2,1,0:T(8,128)(2,1)} %cached.3, bf16[1,2,512,128]{3,2,1,0:T(8,128)(2,1)} %get-tuple-element.4.fresh, bf16[1,64,1280]{2,1,0:T(8,128)(2,1)} %get-tuple-element.5.hidden), custom_call_target="tpu_custom_call" | custom-call | tf_op jit(solution)/shard_map/pallas_call | solution.py:781

commit v3 on v2

--- a/solution.py
+++ b/solution.py
@@ -496,6 +496,8 @@
             if k == 4:
                 ring_stage(DOWN, 3)
                 ring_stage(REST, 3)
+                for d in (1, 3, 2):
+                    x_pass_on(out_piece, 1, d)
             top, weighted = None, None
             lhs = left_side(k) if k < 4 else None
             for n in range(CHUNKS):
@@ -522,8 +524,6 @@
     finish(FRONT)
     for copy in front_over_y(4):
         go(copy)
-    for d in (1, 3, 2):
-        x_pass_on(out_piece, 1, d)
     for n in range(3):
         for d in (1, 3, 2):
             x_pass_on(attended_piece(n), 2 + n, d)
@@ -568,27 +568,38 @@
         at -= GATE_FRONT
         return lambda zz, yy: l_rest[zz, yy, :, at : at + HQ]
 
-    def assemble_ff(p, carry):
+    def put_up(b):
+        def put(rows, value):
+            g_ff[b, rows, 0:HQ] = value
+
+        return put
+
+    def put_gate(b):
+        def put(rows, value):
+            g_ff[b, rows, HQ : 2 * HQ] = value
+
+        return put
+
+    def put_down(rows, value):
+        g_down[rows, :] = value
+
+    def assemble_front(p, carry):
         for b in range(FF // HQ):
-
-            def put_up(rows, value, b=b):
-                g_ff[b, rows, 0:HQ] = value
-
-            def put_gate(rows, value, b=b):
-                g_ff[b, rows, HQ : 2 * HQ] = value
-
-            assemble(p, lambda zz, yy, b=b: l_front[zz, yy, :, b * HQ : (b + 1) * HQ], put_up)
-            assemble(p, gate_block(b), put_gate)
-
-        def put_down(rows, value):
-            g_down[rows, :] = value
-
+            assemble(p, lambda zz, yy, b=b: l_front[zz, yy, :, b * HQ : (b + 1) * HQ], put_up(b))
+        for b in range(GATE_FRONT // HQ):
+            assemble(p, gate_block(b), put_gate(b))
+        return carry
+
+    def assemble_rest(p, carry):
+        for b in range(GATE_FRONT // HQ, FF // HQ):
+            assemble(p, gate_block(b), put_gate(b))
         assemble(p, lambda zz, yy: l_down[zz, yy], put_down)
         return carry
 
+    lax.fori_loop(0, D // (2 * SHARD), assemble_front, 0)
     finish(DOWN)
     finish(REST)
-    lax.fori_loop(0, D // (2 * SHARD), assemble_ff, 0)
+    lax.fori_loop(0, D // (2 * SHARD), assemble_rest, 0)
 
     s_up_row = wide_row(s_up, FF // HQ)
     s_gate_row = wide_row(s_gate, FF // HQ)

time: 85.1 us -> 83.4 us (0.980)
  Pallas kernels: 83.7 us -> 82 us
    pallas_call x1, Pallas kernels: 80.4 us -> 78.7 us  [per_device(): pl.pallas_call(layer_kernel, out_shape=(jax.ShapeDtypeStruct((1, OWN, D),...]
where the time goes in v3:
time: 83.4 us; the launch traced here: 83.2 us
  Pallas kernels  82 us (98%)
  between operations  1.29 us (2%)
    pallas_call x1, Pallas kernels, per_device(): pl.pallas_call(layer_kernel, out_shape=(jax.ShapeDtypeStruct((1, OWN, D),...  78.7 us
    pallas_call x1, Pallas kernels, per_device(): pl.pallas_call(append_kernel, out_shape=(jax.ShapeDtypeStruct((1, OWN, D)...  3.26 us

profile of v3, /device:TPU:1, one launch (start us, length us, event | category | flops | bytes accessed | tf_op | source)
XLA Modules:
  0.0 83.2 jit_solution(12346477975449681720)
XLA Ops:
  1.3 78.7 %shard_map.149 = (bf16[1,64,1280]{2,1,0:T(8,128)(2,1)}, bf16[1,2,512,128]{3,2,1,0:T(8,128)(2,1)}) custom-call(s32[1]{0:T(128)S(6)} %copy.16.lengths, bf16[1,64,1280]{2,1,0:T(8,128)(2,1)} %hidden.1, bf16[1,2,4,128]{3,2,1,0:T(4,128)(2,1)} %sinks.1, bf16[1,2,4608,128]{3,2,1,0:T(8,128)(2,1)} %cached.3, bf16[3,40,128]{2,1,0:T(8,128)(2,1)} %bitcast.9, ...), custom_call_target="tpu_custom_call" | custom-call | tf_op jit(solution)/shard_map/pallas_call | solution.py:708
  80.0 3.3 %shard_map.150 = (bf16[1,64,1280]{2,1,0:T(8,128)(2,1)}, bf16[1,2,4608,128]{3,2,1,0:T(8,128)(2,1)}) custom-call(s32[1]{0:T(128)S(6)} %copy.16.lengths, bf16[1,2,4608,128]{3,2,1,0:T(8,128)(2,1)} %cached.3, bf16[1,2,512,128]{3,2,1,0:T(8,128)(2,1)} %get-tuple-element.4.fresh, bf16[1,64,1280]{2,1,0:T(8,128)(2,1)} %get-tuple-element.5.hidden), custom_call_target="tpu_custom_call" | custom-call | tf_op jit(solution)/shard_map/pallas_call | solution.py:792

commit v4 on v3

--- a/solution.py
+++ b/solution.py
@@ -372,6 +372,8 @@
             remote(
                 piece, piece, qkv_send.at[d, n], qkv_recv.at[d, n], along_y[d]
             ).wait_recv()
+    ring_stage(DOWN, 2)
+    ring_stage(REST, 2)
     for n in (0, 1, 7):
         for copy in front_over_y(n):
             go(copy)
@@ -413,8 +415,6 @@
         return carry
 
     lax.fori_loop(0, TOK // PAIR, project, 0)
-    ring_stage(DOWN, 2)
-    ring_stage(REST, 2)
     ring_stage(FRONT, 3)
     for n in (2, 6):
         for copy in front_over_y(n):
@@ -494,10 +494,11 @@
                     for copy in front_over_y(n):
                         go(copy)
             if k == 4:
+                for d in (1, 3, 2):
+                    x_pass_on(out_piece, 1, d)
+            if k == 3:
                 ring_stage(DOWN, 3)
                 ring_stage(REST, 3)
-                for d in (1, 3, 2):
-                    x_pass_on(out_piece, 1, d)
             top, weighted = None, None
             lhs = left_side(k) if k < 4 else None
             for n in range(CHUNKS):
@@ -551,8 +552,9 @@
         if n == 0:
             for d in (1, 3, 2):
                 x_pass_on(attended_piece(3), 5, d)
-    ring_stage(DOWN, 4)
-    ring_stage(REST, 4)
+        if n == 0:
+            ring_stage(DOWN, 4)
+            ring_stage(REST, 4)
 
     for n in range(ZC):
         for d in (1, 2, 3):

time: 83.4 us -> 82.6 us (level)
  no operation moved by 1% of the time
where the time goes in v4:
time: 82.6 us; the launch traced here: 82.4 us
  Pallas kernels  81.2 us (98%)
  between operations  1.29 us (2%)
    pallas_call x1, Pallas kernels, per_device(): pl.pallas_call(layer_kernel, out_shape=(jax.ShapeDtypeStruct((1, OWN, D),...  77.9 us
    pallas_call x1, Pallas kernels, per_device(): pl.pallas_call(append_kernel, out_shape=(jax.ShapeDtypeStruct((1, OWN, D)...  3.26 us

profile of v4, /device:TPU:1, one launch (start us, length us, event | category | flops | bytes accessed | tf_op | source)
XLA Modules:
  0.0 82.4 jit_solution(8847228667324305990)
XLA Ops:
  1.3 77.9 %shard_map.149 = (bf16[1,64,1280]{2,1,0:T(8,128)(2,1)}, bf16[1,2,512,128]{3,2,1,0:T(8,128)(2,1)}) custom-call(s32[1]{0:T(128)S(6)} %copy.16.lengths, bf16[1,64,1280]{2,1,0:T(8,128)(2,1)} %hidden.1, bf16[1,2,4,128]{3,2,1,0:T(4,128)(2,1)} %sinks.1, bf16[1,2,4608,128]{3,2,1,0:T(8,128)(2,1)} %cached.3, bf16[3,40,128]{2,1,0:T(8,128)(2,1)} %bitcast.9, ...), custom_call_target="tpu_custom_call" | custom-call | tf_op jit(solution)/shard_map/pallas_call | solution.py:710
  79.2 3.3 %shard_map.150 = (bf16[1,64,1280]{2,1,0:T(8,128)(2,1)}, bf16[1,2,4608,128]{3,2,1,0:T(8,128)(2,1)}) custom-call(s32[1]{0:T(128)S(6)} %copy.16.lengths, bf16[1,2,4608,128]{3,2,1,0:T(8,128)(2,1)} %cached.3, bf16[1,2,512,128]{3,2,1,0:T(8,128)(2,1)} %get-tuple-element.4.fresh, bf16[1,64,1280]{2,1,0:T(8,128)(2,1)} %get-tuple-element.5.hidden), custom_call_target="tpu_custom_call" | custom-call | tf_op jit(solution)/shard_map/pallas_call | solution.py:794
